TPU v7x, 128 devices: a whole 4x4x4 slice. The times are simulated.
128 devices in a mesh: space: 16 (over x, z), chan: 8 (over y, core).
Axes of the slice: x: 4, y: 4, z: 4, core: 2. Of those that a mesh axis runs over, the one named last changes fastest.
Arguments:
- volume: bfloat16 [64, 16, 16, 512], P('space', 'chan'), may hold values from -6 to 6
- w_first: bfloat16 [27, 512, 1024], P(None, 'space', 'chan'), may hold values from -0.0546875 to 0.0546875
- b_first: float32 [1024], P('chan'), may hold values from -3 to 3
- w_second: bfloat16 [27, 1024, 1024], P(None, 'space', 'chan'), may hold values from -0.0390625 to 0.0390625
- b_second: float32 [1024], P('chan'), may hold values from -3 to 3
- cotangent: bfloat16 [64, 16, 16, 1024], P('space', None, None, 'chan'), may hold values from -6 to 6
Outputs:
- features: bfloat16 [64, 16, 16, 1024], P('space', None, None, 'chan')
- grad_input: float32 [64, 16, 16, 512], P('space', 'chan')
- grad_first: float32 [27, 512, 1024], P(None, 'space', 'chan')
- grad_second: float32 [27, 1024, 1024], P(None, 'space', 'chan')
All inputs are finite; a program needn't handle non-finite values.
Results may differ from a plain program's by a relative error of at most 0.0054.
Values may be sent and summed in bfloat16 or wider, within the bound.
A program may use at most 512 MiB of HBM per device.

v0:
```python
import jax
import jax.numpy as jnp
from jax import lax
from jax.sharding import PartitionSpec as P


def with_halo(cells, sides, width):
    for axis, dim in sides:
        count = lax.axis_size(axis)
        ends = count - 1
        head = lax.slice_in_dim(cells, 0, width, axis=dim)
        tail = lax.slice_in_dim(cells, cells.shape[dim] - width, cells.shape[dim], axis=dim)
        cells = jnp.concatenate(
            [
                lax.ppermute(tail, axis, [(i, (i + 1) % count) for i in range(ends)]),
                cells,
                lax.ppermute(head, axis, [((i + 1) % count, i) for i in range(ends)]),
            ],
            axis=dim,
        )
    return cells


def pad_sides(field):
    return jnp.pad(field, ((0, 0), (1, 1), (1, 1), (0, 0)))


def silu_slope(values):
    sigma = jax.nn.sigmoid(values)
    return sigma * (1.0 + values * (1.0 - sigma))


def convolve(padded, weights):
    span_x = padded.shape[0] - 2
    span_y = padded.shape[1] - 2
    span_z = padded.shape[2] - 2
    summed = jnp.zeros((span_x * span_y * span_z, weights.shape[2]), jnp.float32)
    for offset in range(27):
        a, b, c = (offset // 9, offset // 3 % 3, offset % 3)
        sliced = padded[a : a + span_x, b : b + span_y, c : c + span_z].reshape(-1, padded.shape[3])
        summed = summed + jnp.dot(sliced, weights[offset], preferred_element_type=jnp.float32)
    return summed.reshape(span_x, span_y, span_z, -1)


def convolve_back(padded, weights):
    span_x = padded.shape[0] - 2
    span_y = padded.shape[1] - 2
    span_z = padded.shape[2] - 2
    summed = jnp.zeros((span_x * span_y * span_z, weights.shape[1]), jnp.float32)
    for offset in range(27):
        a, b, c = (offset // 9, offset // 3 % 3, offset % 3)
        sliced = padded[
            2 - a : 2 - a + span_x, 2 - b : 2 - b + span_y, 2 - c : 2 - c + span_z
        ].reshape(-1, padded.shape[3])
        summed = summed + jnp.dot(sliced, weights[offset].T, preferred_element_type=jnp.float32)
    return summed.reshape(span_x, span_y, span_z, -1)


def weight_grad(padded, grads):
    span_x = grads.shape[1]
    span_y = grads.shape[2]
    span_z = grads.shape[3]
    flat_grads = grads.reshape(-1, grads.shape[4])
    results = []
    for offset in range(27):
        a, b, c = (offset // 9, offset // 3 % 3, offset % 3)
        sliced = padded[:, a : a + span_x, b : b + span_y, c : c + span_z].reshape(
            -1, padded.shape[4]
        )
        results.append(jnp.dot(sliced.T, flat_grads, preferred_element_type=jnp.float32))
    return jnp.stack(results)


def local(volume, w_first, b_first, w_second, b_second, cotangent):
    full_first, full_second = (
        lax.all_gather(w_first, "space", axis=1, tiled=True),
        lax.all_gather(w_second, "space", axis=1, tiled=True),
    )
    slab_rows = lax.all_gather(volume, "chan", axis=1, tiled=True)
    rimmed = with_halo(slab_rows, (("space", 0),), 1)
    padded_in = pad_sides(rimmed)
    pre_first = convolve(padded_in, full_first) + b_first
    hidden = jax.nn.silu(pre_first).astype(jnp.bfloat16)
    hidden_rimmed = with_halo(hidden, (("space", 0),), 1)
    padded_hidden = pad_sides(lax.all_gather(hidden_rimmed, "chan", axis=3, tiled=True))
    pre_second = convolve(padded_hidden, full_second) + b_second
    features = jax.nn.silu(pre_second).astype(jnp.bfloat16)
    adjoint_out = (cotangent.astype(jnp.float32) * silu_slope(pre_second)).astype(jnp.bfloat16)
    padded_adjoint = pad_sides(with_halo(adjoint_out, (("space", 0),), 1))
    hidden_terms = convolve_back(padded_adjoint, full_second)
    hidden_adjoint = lax.psum_scatter(hidden_terms, "chan", scatter_dimension=3, tiled=True)
    adjoint_first = (hidden_adjoint * silu_slope(pre_first)).astype(jnp.bfloat16)
    padded_first = pad_sides(with_halo(adjoint_first, (("space", 0),), 1))
    input_terms = convolve_back(padded_first, full_first)
    grad_input = lax.psum_scatter(input_terms, "chan", scatter_dimension=1, tiled=True)
    parts_first = weight_grad(padded_in[None], adjoint_first[None])
    parts_second = weight_grad(padded_hidden[None], adjoint_out[None])
    grad_first, grad_second = (
        lax.psum_scatter(parts_first, "space", scatter_dimension=1, tiled=True),
        lax.psum_scatter(parts_second, "space", scatter_dimension=1, tiled=True),
    )
    return (features, grad_input, grad_first, grad_second)


def solution(mesh):
    return jax.shard_map(
        local,
        mesh=mesh,
        in_specs=(
            P("space", "chan", None, None),
            P(None, "space", "chan"),
            P("chan"),
            P(None, "space", "chan"),
            P("chan"),
            P("space", None, None, "chan"),
        ),
        out_specs=(
            P("space", None, None, "chan"),
            P("space", "chan", None, None),
            P(None, "space", "chan"),
            P(None, "space", "chan"),
        ),
        check_vma=False,
    )
```

profile of v0, /device:TPU:0, one launch (start us, length us, event | category | flops | bytes accessed | tf_op | source)
XLA Modules:
  0.0 761.8 jit_solution(17820070867058766720)
XLA Ops:
  8.7 26.9 %all-gather.5.cloned.1.call-done = bf16[4,16,16,512]{3,2,1,0:T(8,128)(2,1)} async-done(((bf16[4,2,16,512]{3,2,1,0:T(8,128)(2,1)}), bf16[4,16,16,512]{3,2,1,0:T(8,128)(2,1)}) %all-gather.5.cloned.1.call-update) | async-done | bytes 1048592 | tf_op jit(solution)/shard_map/all_gather | solution.py:79
  36.7 3.5 collective-permute-start
  41.5 4.7 collective-permute-done
  46.2 4.1 collective-permute-done.1
  53.2 3.3 fusion.178
  56.5 8.7 %fusion.177 = (bf16[4,16,16,512]{3,2,1,0:T(8,128)(2,1)}, bf16[4,16,16,512]{3,2,1,0:T(8,128)(2,1)}, bf16[4,16,16,512]{3,2,1,0:T(8,128)(2,1)}, bf16[4,16,16,512]{3...) fusion(bf16[6,18,18,512]{3,2,1,0:T(8,128)(2,1)S(1)} %select_max, ...), kind=kLoop, calls=%fused_computation.366 | loop fusion | bytes 39845888 | tf_op jit(solution)/shard_map/slice | solution.py:40
  65.1 27.0 %all-gather.7.cloned.1.call-done = bf16[27,512,128]{2,1,0:T(8,128)(2,1)} async-done(((bf16[27,32,128]{2,1,0:T(8,128)(2,1)}), bf16[27,512,128]{2,1,0:T(8,128)(2,1)}) %all-gather.7.cloned.1.call-update) | async-done | bytes 3538960 | tf_op jit(solution)/shard_map/all_gather | solution.py:76
  116.4 4.3 collective-permute-done.3
  122.1 33.8 %all-gather.9.cloned.1.call-done = bf16[6,16,16,1024]{3,2,1,0:T(8,128)(2,1)} async-done(((bf16[6,16,16,128]{3,2,1,0:T(8,128)(2,1)}), bf16[6,16,16,1024]{3,2,1,0:T(8,128)(2,1)}) %all-gather.9.cloned.1.call-update) | async-done | bytes 3145744 | tf_op jit(solution)/shard_map/all_gather | solution.py:85
  156.0 11.9 %pad_slice_fusion.1 = (bf16[4,16,16,1024]{3,2,1,0:T(8,128)(2,1)}, bf16[4,16,16,1024]{3,2,1,0:T(8,128)(2,1)}, bf16[4,16,16,1024]{3,2,1,0:T(8,128)(2,1)}, bf16[4,1...) fusion(bf16[6,16,16,1024]{3,2,1,0:T(8,128)(2,1)} %all-gather.9., ...), kind=kLoop, calls=%fused_computation.2 | loop fusion | bytes 26214400 | tf_op jit(solution)/shard_map/slice | solution.py:40
  167.9 14.2 %pad_slice_fusion = (bf16[4,16,16,1024]{3,2,1,0:T(8,128)(2,1)}, bf16[4,16,16,1024]{3,2,1,0:T(8,128)(2,1)}, bf16[4,16,16,1024]{3,2,1,0:T(8,128)(2,1)}, bf16[4,16,...) fusion(bf16[6,16,16,1024]{3,2,1,0:T(8,128)(2,1)S(1)} %copy-done.2), kind=kLoop, calls=%fused_computation.1 | loop fusion | bytes 42991616 | tf_op jit(solution)/shard_map/slice | solution.py:40
  182.1 42.0 %all-gather.11.cloned.1.call-done = bf16[27,1024,128]{2,1,0:T(8,128)(2,1)} async-done(((bf16[27,64,128]{2,1,0:T(8,128)(2,1)}), bf16[27,1024,128]{2,1,0:T(8,128)(2,1)}) %all-gather.11.cloned.1.call-update) | async-done | bytes 7077904 | tf_op jit(solution)/shard_map/all_gather | solution.py:77
  331.3 35.7 %add_add_fusion = f32[1024,1024]{1,0:T(8,128)} fusion(f32[1024,1024]{1,0:T(8,128)} %fusion.121, f32[1024,1024]{1,0:T(8,128)} %fusion.120, f32[1024,1024]{1,0:T(8,128)} %fusion.119, f32[1024,1024]{1,0:T(8,128)} %fusion.118, f32[1024,1024]{1,0:T(8,128)} %fusion.117, f32[1024,1024]{1,0:T(8,128)} %fusion.116, f32[1024,1024]{1,0:T(8,128)} %fusion.115, ...), kind=kOutput, calls=%fused_computation.32 | convolution fusion | flops 295698432 | bytes 113770496 | tf_op jit(solution)/shard_map/dot_general | solution.py:55
  369.2 4.3 fusion.176
  373.4 8.0 %fusion.175 = (bf16[1,4,16,16,512]{4,3,2,1,0:T(8,128)(2,1)S(1)}, bf16[1,4,16,16,512]{4,3,2,1,0:T(8,128)(2,1)}, bf16[1,4,16,16,512]{4,3,2,1,0:T(8,128)(2,1)}, bf1...) fusion(bf16[1,6,18,18,512]{4,3,2,1,0:T(8,128)(2,1)S(1)} %fusion.403), kind=kLoop, calls=%fused_computation.364 | loop fusion | bytes 39845888 | tf_op jit(solution)/shard_map/slice | solution.py:67
  381.5 26.3 %reduce-scatter.7.cloned.1.call-done = f32[4,16,16,128]{3,2,1,0:T(8,128)} async-done(((f32[4,16,16,1024]{3,2,1,0:T(8,128)}), f32[4,16,16,128]{3,2,1,0:T(8,128)}) %reduce-scatter.7.cloned.1.call-update) | async-done | bytes 524304 | tf_op jit(solution)/shard_map/reduce_scatter | solution.py:91
  409.2 3.6 collective-permute-start.6
  478.9 20.0 %add_add_fusion.1 = f32[1024,512]{1,0:T(8,128)} fusion(f32[1024,512]{1,0:T(8,128)} %fusion.171, f32[1024,512]{1,0:T(8,128)} %fusion.169, f32[1024,512]{1,0:T(8,128)} %fusion.167, f32[1024,512]{1,0:T(8,128)} %fusion.165, f32[1024,512]{1,0:T(8,128)} %fusion.162, f32[1024,512]{1,0:T(8,128)} %fusion.160, f32[1024,512]{1,0:T(8,128)} %fusion.158, ...), kind=kOutput, calls=%fused_computation.38 | convolution fusion | flops 147849216 | bytes 57016320 | tf_op jit(solution)/shard_map/dot_general | solution.py:55
  505.5 4.4 pad_bitcast_fusion
  509.9 8.4 %fusion.174 = (bf16[1,4,16,16,1024]{4,3,2,1,0:T(8,128)(2,1)}, bf16[1,4,16,16,1024]{4,3,2,1,0:T(8,128)(2,1)}, bf16[1,4,16,16,1024]{4,3,2,1,0:T(8,128)(2,1)}, bf16...) fusion(bf16[1,6,18,18,1024]{4,3,2,1,0:T(8,128)(2,1)S(1)} %pad_b, ...), kind=kLoop, calls=%fused_computation.363 | loop fusion | bytes 33554432 | tf_op jit(solution)/shard_map/slice | solution.py:67
  518.3 15.7 %fusion.173 = (bf16[1,4,16,16,1024]{4,3,2,1,0:T(8,128)(2,1)S(1)}, bf16[1,4,16,16,1024]{4,3,2,1,0:T(8,128)(2,1)}, bf16[1,4,16,16,1024]{4,3,2,1,0:T(8,128)(2,1)}, ...) fusion(bf16[1,6,18,18,1024]{4,3,2,1,0:T(8,128)(2,1)S(1)} %pad_b, ...), kind=kLoop, calls=%fused_computation.362 | loop fusion | bytes 79691776 | tf_op jit(solution)/shard_map/slice | solution.py:67
  534.1 3.3 fusion.39
  582.2 69.0 %reduce-scatter.9.cloned.1.call-done = f32[27,32,128]{2,1,0:T(8,128)} async-done(((f32[27,512,128]{2,1,0:T(8,128)}), f32[27,32,128]{2,1,0:T(8,128)}) %reduce-scatter.9.cloned.1.call-update) | async-done | bytes 442384 | tf_op jit(solution)/shard_map/reduce_scatter | solution.py:99
  651.2 103.5 %reduce-scatter.11.cloned.1.call-done = f32[27,64,128]{2,1,0:T(8,128)} async-done(((f32[27,1024,128]{2,1,0:T(8,128)}), f32[27,64,128]{2,1,0:T(8,128)}) %reduce-scatter.11.cloned.1.call-update) | async-done | bytes 884752 | tf_op jit(solution)/shard_map/reduce_scatter | solution.py:100
  (422 shorter events, 258.5 us)
Async XLA Ops:
  7.2 28.4 %all-gather.5.cloned.1.call-start = ((), (), s32[]{:S(2)}) async-start(), calls=%async_computation.3 | async-start | bytes 1179648 | tf_op jit(solution)/shard_map/all_gather | solution.py:79
  7.9 84.2 %all-gather.7.cloned.1.call-start = ((), (), s32[]{:S(2)}) async-start(), calls=%async_computation.4 | async-start | bytes 3760128 | tf_op jit(solution)/shard_map/all_gather | solution.py:76
  8.6 147.3 %all-gather.9.cloned.1.call-start = ((), (), s32[]{:S(2)}) async-start(), calls=%async_computation.5 | async-start | bytes 3538944 | tf_op jit(solution)/shard_map/all_gather | solution.py:85
  35.6 16.4 %copy-start.4 = (bf16[4,16,16,512]{3,2,1,0:T(8,128)(2,1)S(1)}, bf16[4,16,16,512]{3,2,1,0:T(8,128)(2,1)}, u32[]{:S(2)}) copy-start(bf16[4,16,16,512]{3,2,1,0:T(8,128)(2,1)} %all-gather.5.cloned.1.call-done) | copy-start | bytes 3145732
  36.7 9.4 %collective-permute-start = (bf16[1,16,16,512]{3,2,1,0:T(8,128)(2,1)S(1)}, bf16[1,16,16,512]{3,2,1,0:T(8,128)(2,1)S(1)}, u32[]{:S(2)}, u32[]{:S(2)}) collective-permute-start(bf16[1,16,16,512]{3,2,1,0:T(8,128)(2,1)S(1)} %get-tuple-element.111), channel_id=1, source_target_pairs={{0,8},{8,16},{16,24},{24,32},{32,40},{40,48},{48,56},{56,64},{64,7... | collective-permute-start | bytes 786440 | tf_op jit(solution)/shard_map/ppermute | solution.py:15
  40.2 10.1 %collective-permute-start.1 = (bf16[1,16,16,512]{3,2,1,0:T(8,128)(2,1)S(1)}, bf16[1,16,16,512]{3,2,1,0:T(8,128)(2,1)S(1)}, u32[]{:S(2)}, u32[]{:S(2)}) collective-permute-start(bf16[1,16,16,512]{3,2,1,0:T(8,128)(2,1)S(1)} %get-tuple-element.112), channel_id=1, source_target_pairs={{8,0},{16,8},{24,16},{32,24},{40,32},{48,40},{56,48},{64,56},{72,6... | collective-permute-start | bytes 786440 | tf_op jit(solution)/shard_map/ppermute | solution.py:17
  111.5 4.9 collective-permute-start.2
  114.5 6.2 collective-permute-start.3
  121.5 102.6 %all-gather.11.cloned.1.call-start = ((), (), s32[]{:S(2)}) async-start(), calls=%async_computation.6 | async-start | bytes 7520256 | tf_op jit(solution)/shard_map/all_gather | solution.py:77
  122.1 285.7 %reduce-scatter.7.cloned.1.call-start = ((), (), s32[]{:S(2)}) async-start(), calls=%async_computation.7 | async-start | bytes 4718592 | tf_op jit(solution)/shard_map/reduce_scatter | solution.py:91
  156.0 11.9 %copy-start.2 = (bf16[6,16,16,1024]{3,2,1,0:T(8,128)(2,1)S(1)}, bf16[6,16,16,1024]{3,2,1,0:T(8,128)(2,1)}, u32[]{:S(2)}) copy-start(bf16[6,16,16,1024]{3,2,1,0:T(8,128)(2,1)} %all-gather.9.cloned.1.call-done) | copy-start | bytes 9437188
  251.9 10.9 %copy-start = (bf16[4,16,16,128]{3,2,1,0:T(8,128)(2,1)}, bf16[4,16,16,128]{3,2,1,0:T(8,128)(2,1)S(1)}, u32[]{:S(2)}) copy-start(bf16[4,16,16,128]{3,2,1,0:T(8,128)(2,1)S(1)} %get-tuple-element.161) | copy-start | bytes 786436
  251.9 7.2 collective-permute-start.4
  255.1 6.2 collective-permute-start.5
  367.1 213.5 %all-reduce.7.cloned.1.call-start = ((), (), s32[]{:S(2)}) async-start(), calls=%async_computation.10 | async-start | bytes 4194304
  373.4 34.4 %copy-start.58 = (f32[1024,128]{1,0:T(8,128)S(1)}, f32[1024,128]{1,0:T(8,128)}, u32[]{:S(2)}) copy-start(f32[1024,128]{1,0:T(8,128)} %copy-done.57) | copy-start | bytes 1572868
  407.8 10.1 %copy-start.80 = (bf16[1,4,16,16,512]{4,3,2,1,0:T(8,128)(2,1)S(1)}, bf16[1,4,16,16,512]{4,3,2,1,0:T(8,128)(2,1)}, u32[]{:S(2)}) copy-start(bf16[1,4,16,16,512]{4,3,2,1,0:T(8,128)(2,1)} %get-tuple-element.82) | copy-start | bytes 3145732
  407.8 10.6 %copy-start.79 = (bf16[1,4,16,16,512]{4,3,2,1,0:T(8,128)(2,1)S(1)}, bf16[1,4,16,16,512]{4,3,2,1,0:T(8,128)(2,1)}, u32[]{:S(2)}) copy-start(bf16[1,4,16,16,512]{4,3,2,1,0:T(8,128)(2,1)} %get-tuple-element.81) | copy-start | bytes 3145732
  409.2 9.7 %copy-start.78 = (bf16[1,4,16,16,512]{4,3,2,1,0:T(8,128)(2,1)S(1)}, bf16[1,4,16,16,512]{4,3,2,1,0:T(8,128)(2,1)}, u32[]{:S(2)}) copy-start(bf16[1,4,16,16,512]{4,3,2,1,0:T(8,128)(2,1)} %get-tuple-element.80) | copy-start | bytes 3145732
  409.2 19.9 %collective-permute-start.6 = (bf16[1,16,16,128]{3,2,1,0:T(8,128)(2,1)S(1)}, bf16[1,16,16,128]{3,2,1,0:T(8,128)(2,1)S(1)}, u32[]{:S(2)}, u32[]{:S(2)}) collective-permute-start(bf16[1,16,16,128]{3,2,1,0:T(8,128)(2,1)S(1)} %get-tuple-element.165), channel_id=1, source_target_pairs={{0,8},{8,16},{16,24},{24,32},{32,40},{40,48},{48,56},{56,64},{64,7... | collective-permute-start | bytes 196616 | tf_op jit(solution)/shard_map/ppermute | solution.py:15
  412.9 19.1 %collective-permute-start.7 = (bf16[1,16,16,128]{3,2,1,0:T(8,128)(2,1)S(1)}, bf16[1,16,16,128]{3,2,1,0:T(8,128)(2,1)S(1)}, u32[]{:S(2)}, u32[]{:S(2)}) collective-permute-start(bf16[1,16,16,128]{3,2,1,0:T(8,128)(2,1)S(1)} %get-tuple-element.166), channel_id=1, source_target_pairs={{8,0},{16,8},{24,16},{32,24},{40,32},{48,40},{56,48},{64,56},{72,6... | collective-permute-start | bytes 196616 | tf_op jit(solution)/shard_map/ppermute | solution.py:17
  498.9 152.4 %reduce-scatter.9.cloned.1.call-start = ((), (), s32[]{:S(2)}) async-start(), calls=%async_computation.8 | async-start | bytes 7520256 | tf_op jit(solution)/shard_map/reduce_scatter | solution.py:99
  505.4 249.3 %reduce-scatter.11.cloned.1.call-start = ((), (), s32[]{:S(2)}) async-start(), calls=%async_computation.9 | async-start | bytes 15040512 | tf_op jit(solution)/shard_map/reduce_scatter | solution.py:100
  518.3 15.8 %copy-start.1 = (bf16[4,16,16,128]{3,2,1,0:T(8,128)(2,1)S(1)}, bf16[4,16,16,128]{3,2,1,0:T(8,128)(2,1)}, u32[]{:S(2)}) copy-start(bf16[4,16,16,128]{3,2,1,0:T(8,128)(2,1)} %copy-done) | copy-start | bytes 786436
  (99 other events, 209.0 us)
Sparse Core Ops, SparseCore 0:
  9.7 25.8 all-gather.4
  37.7 54.4 all-gather.6
  121.6 34.2 all-gather.8
  158.0 66.0 all-gather.10
  367.2 40.5 reduce-scatter.6
  499.0 65.5 all-reduce.6
  568.6 82.5 reduce-scatter.8
  655.7 98.9 reduce-scatter.10
where the time goes:
time: 768 us; the launch traced here: 762 us
  waiting for transfers between devices  346 us (45%)
  matrix products  277 us (36%)
  local copies, waits for them, and re-layouts  93.9 us (12%)
  starting transfers between devices  19.4 us (3%)
  between operations  16.7 us (2%)
  other arithmetic  8.64 us (1%)
    dot_general x54, matrix products, convolve_back(): jnp.dot(sliced, weights[offset].T, preferred_element_type=jnp.float32)  172 us
    reduce_scatter x1, waiting for transfers between devices, local(): lax.psum_scatter(parts_second, 'space', scatter_dimension=1, tiled=True)  104 us
    reduce_scatter x1, waiting for transfers between devices, local(): lax.psum_scatter(parts_first, 'space', scatter_dimension=1, tiled=True)  69 us
    dot_general x54, matrix products, weight_grad(): jnp.dot(sliced.T, flat_grads, preferred_element_type=jnp.float32)  63.5 us
    all_gather x1, waiting for transfers between devices, local(): lax.all_gather(w_second, 'space', axis=1, tiled=True)  42 us
    dot_general x54, matrix products, convolve(): jnp.dot(sliced, weights[offset], preferred_element_type=jnp.float32)  41.4 us
    slice x4, local copies, waits for them, and re-layouts, convolve(): padded[a:a + span_x, b:b + span_y, c:c + span_z]  38.1 us
    slice x4, local copies, waits for them, and re-layouts, weight_grad(): padded[:, a:a + span_x, b:b + span_y, c:c + span_z]  36.4 us
  transfers between devices with their start and end apart: 16, of which 12 were waited for; matrix products, arithmetic and copies ran while one was open for 20% of the time, Pallas kernels for 0%

commit v1 on v0

v1 whole, which is shorter than its diff:
```python
import functools

import jax
import jax.numpy as jnp
from jax import lax
from jax.experimental import pallas as pl
from jax.experimental.pallas import tpu as pltpu
from jax.sharding import PartitionSpec as P

MESH = pl.DeviceIdType.MESH
BF = jnp.bfloat16
F32 = jnp.float32
VMEM_BYTES = 63 * 1024 * 1024
RING = (1, 3, 2)
HALVES = ((0, 14), (14, 13))


def place():
    s = lax.axis_index("space")
    c = lax.axis_index("chan")
    return s, c, lax.div(s, 4), lax.rem(s, 4), lax.div(c, 2), lax.rem(c, 2)


def send(src, dst, send_sem, recv_sem, target):
    return pltpu.make_async_remote_copy(
        src_ref=src,
        dst_ref=dst,
        send_sem=send_sem,
        recv_sem=recv_sem,
        device_id=target,
        device_id_type=MESH,
    )


def greet(s, c, x, z):
    barrier = pltpu.get_barrier_semaphore()

    def signal(space, chan):
        pl.semaphore_signal(barrier, inc=1, device_id=(space, chan), device_id_type=MESH)

    for d in (1, 2, 3):
        signal(lax.rem(x + d, 4) * 4 + z, c)
        signal(x * 4 + lax.rem(z + d, 4), c)
    for d in range(1, 8):
        signal(s, lax.rem(c + d, 8))

    @pl.when(s > 0)
    def _():
        signal(s - 1, c)

    @pl.when(s < 15)
    def _():
        signal(s + 1, c)

    inner = jnp.where(s > 0, 1, 0) + jnp.where(s < 15, 1, 0)
    pl.semaphore_wait(barrier, 13 + inner)


class Halo:
    def __init__(self, s, c, low_src, high_src, low_dst, high_dst, send_sem, recv_sem):
        self.s = s
        self.down = send(low_src, high_dst, send_sem.at[0], recv_sem.at[0], (jnp.maximum(s - 1, 0), c))
        self.up = send(high_src, low_dst, send_sem.at[1], recv_sem.at[1], (jnp.minimum(s + 1, 15), c))

    def start_down(self):
        pl.when(self.s > 0)(self.down.start)

    def start_up(self):
        pl.when(self.s < 15)(self.up.start)

    def start(self):
        self.start_down()
        self.start_up()

    def wait_recv(self):
        pl.when(self.s < 15)(self.down.wait_recv)
        pl.when(self.s > 0)(self.up.wait_recv)

    def wait_send(self):
        pl.when(self.s > 0)(self.down.wait_send)
        pl.when(self.s < 15)(self.up.wait_send)


class Gather:
    def __init__(self, own, full, x, z, c, send_sem, recv_sem):
        self.own, self.full, self.x, self.z, self.c = own, full, x, z, c
        self.send_sem, self.recv_sem = send_sem, recv_sem

    def copy(self, half, first, second, source_own, stage):
        k0, nk = HALVES[half]
        back1, back2 = (first, second)
        if stage == 1:
            o1, o2 = 0, 0
        else:
            o1, o2 = back1, 0
        if half == 0:
            ox, oz = lax.rem(self.x + 4 - o1, 4), self.z
            tx = lax.rem(self.x + back1, 4) if stage == 1 else self.x
            tz = self.z if stage == 1 else lax.rem(self.z + back2, 4)
        else:
            ox, oz = self.x, lax.rem(self.z + 4 - o1, 4)
            tz = lax.rem(self.z + back1, 4) if stage == 1 else self.z
            tx = self.x if stage == 1 else lax.rem(self.x + back2, 4)
        dst = self.full.at[pl.ds(k0, nk), ox, oz]
        src = self.own.at[pl.ds(k0, nk)] if source_own else dst
        index = first * 4 + second
        return send(
            src,
            dst,
            self.send_sem.at[half, index],
            self.recv_sem.at[half, index],
            (tx * 4 + tz, self.c),
        )

    def arrived(self, half, first, second):
        k0, nk = HALVES[half]
        if half == 0:
            ox, oz = lax.rem(self.x + 4 - first, 4), lax.rem(self.z + 4 - second, 4)
        else:
            oz, ox = lax.rem(self.z + 4 - first, 4), lax.rem(self.x + 4 - second, 4)
        region = self.full.at[pl.ds(k0, nk), ox, oz]
        index = first * 4 + second
        send(
            region,
            region,
            self.send_sem.at[half, index],
            self.recv_sem.at[half, index],
            (lax.rem(self.x + 1, 4) * 4 + self.z, self.c),
        ).wait_recv()

    def start_own(self):
        for d in RING:
            for half in (0, 1):
                self.copy(half, d, 0, True, 1).start()
        for d in RING:
            for half in (0, 1):
                self.copy(half, 0, d, True, 2).start()

    def forward(self, d):
        for half in (0, 1):
            self.arrived(half, d, 0)
            for e in RING:
                self.copy(half, d, e, False, 2).start()

    def wait_second(self):
        for d in range(4):
            for e in RING:
                for half in (0, 1):
                    self.arrived(half, d, e)

    def wait_send(self):
        for half in (0, 1):
            for d in RING:
                self.copy(half, d, 0, True, 1).wait_send()
            for d in range(4):
                for e in RING:
                    self.copy(half, d, e, d == 0, 2).wait_send()


class ChanGather:
    def __init__(self, region, s, y, core, y_send, y_recv, c_send, c_recv):
        self.region, self.s, self.y, self.core = region, s, y, core
        self.sems = (y_send, y_recv, c_send, c_recv)

    def to_y(self, d):
        block = self.region(self.y * 2 + self.core)
        y_send, y_recv, _, _ = self.sems
        return send(
            block, block, y_send.at[d], y_recv.at[d], (self.s, lax.rem(self.y + d, 4) * 2 + self.core)
        )

    def from_y(self, d):
        block = self.region(lax.rem(self.y + 4 - d, 4) * 2 + self.core)
        y_send, y_recv, _, _ = self.sems
        return send(
            block, block, y_send.at[d], y_recv.at[d], (self.s, lax.rem(self.y + d, 4) * 2 + self.core)
        )

    def sibling(self, d, other):
        core = (1 - self.core) if other else self.core
        block = self.region(lax.rem(self.y + 4 - d, 4) * 2 + core)
        _, _, c_send, c_recv = self.sems
        return send(block, block, c_send.at[d], c_recv.at[d], (self.s, self.y * 2 + 1 - self.core))

    def start_own(self):
        for d in RING:
            self.to_y(d).start()
        self.sibling(0, False).start()

    def forward(self):
        for d in RING:
            self.from_y(d).wait_recv()
            self.sibling(d, False).start()

    def finish(self):
        for d in range(4):
            self.sibling(d, True).wait_recv()

    def wait_send(self):
        for d in RING:
            self.to_y(d).wait_send()
        for d in range(4):
            self.sibling(d, False).wait_send()


def z_mask(last):
    row = lax.broadcasted_iota(jnp.int32, (256, 128), 0)
    return lax.rem(row, 16) != (15 if last else 0)


def behind(v):
    return jnp.where(z_mask(False), pltpu.roll(v, 1, 0), 0.0)


def ahead(v):
    return jnp.where(z_mask(True), pltpu.roll(v, 255, 0), 0.0)


def slope_of(v):
    sigma = jax.nn.sigmoid(v)
    return sigma * (1.0 + v * (1.0 - sigma))


def stack_shifts(v, xp, stacked, x0, y0, flipped):
    for k, shifted in enumerate((ahead(v), v, behind(v))):
        stacked[xp + x0, y0 : y0 + 16, :, k * 128 : (k + 1) * 128] = shifted.astype(BF).reshape(16, 16, 128)
        flipped[k * 128 : (k + 1) * 128, xp * 256 : (xp + 1) * 256] = shifted.T.astype(BF)


def dot(a, b):
    return jnp.dot(a, b, preferred_element_type=F32)


def convolve_pair(load, load_w, planes, acc):
    def step(j, _):
        a, b = lax.div(j, 3), lax.rem(j, 3)
        rows = jnp.concatenate([load(p + a, b) for p in planes], axis=0)
        filters = jnp.concatenate([load_w(3 * j + k) for k in range(3)], axis=1)
        acc[...] += dot(rows, filters)
        return 0

    acc[...] = jnp.zeros_like(acc)
    lax.fori_loop(0, 9, step, 0)


def plane_of(acc, index):
    rows = slice(index * 256, (index + 1) * 256)
    return behind(acc[rows, 0:128]) + acc[rows, 128:256] + ahead(acc[rows, 256:384])


def forward_kernel(
    vol, w1, b1, w2, b2, cot,
    feat, stacked, flipped, slope, u1_out, u2_out, w1_out, w2_out,
    u1, u2, f1, f2, acc,
    ag1_s, ag1_r, ag2_s, ag2_r, halo_s, halo_r, hh_s, hh_r, y_s, y_r, c_s, c_r, hy_s, hy_r, hc_s, hc_r, loc,
):
    s, c, x, z, y, core = place()
    u1[0] = jnp.zeros((18, 16, 512), BF)
    u1[5] = jnp.zeros((18, 16, 512), BF)
    for row in (0, 17):
        u1[1:5, row] = jnp.zeros((4, 16, 512), BF)

    def clear(b, _):
        u2[b, 0] = jnp.zeros((18, 16, 128), BF)
        u2[b, 5] = jnp.zeros((18, 16, 128), BF)
        for row in (0, 17):
            u2[b, 1:5, row] = jnp.zeros((4, 16, 128), BF)
        return 0

    lax.fori_loop(0, 8, clear, 0)
    rows_of = lambda cb: u1.at[:, pl.ds(1 + 2 * cb, 2)]
    locals_ = [
        pltpu.make_async_copy(vol, u1.at[1:5, pl.ds(1 + 2 * c, 2)], loc.at[0]),
        pltpu.make_async_copy(w1, f1.at[:, x, z], loc.at[1]),
        pltpu.make_async_copy(w2, f2.at[:, x, z], loc.at[2]),
    ]
    for copy in locals_:
        copy.start()
    greet(s, c, x, z)

    first = Gather(w1, f1, x, z, c, ag1_s, ag1_r)
    second = Gather(w2, f2, x, z, c, ag2_s, ag2_r)
    halo = Halo(
        s, c, vol.at[0], vol.at[3],
        u1.at[0, pl.ds(1 + 2 * c, 2)], u1.at[5, pl.ds(1 + 2 * c, 2)], halo_s, halo_r,
    )
    rows = ChanGather(rows_of, s, y, core, y_s, y_r, c_s, c_r)
    halo.start()
    first.start_own()
    locals_[0].wait()
    halo.wait_recv()
    rows.start_own()
    for d in RING:
        first.forward(d)
    second.start_own()
    rows.forward()
    rows.finish()
    locals_[1].wait()
    locals_[2].wait()
    first.wait_second()
    save_u1 = pltpu.make_async_copy(u1, u1_out, loc.at[3])
    save_w1 = pltpu.make_async_copy(f1, w1_out, loc.at[4])
    save_u1.start()
    save_w1.start()

    hidden_halo = Halo(
        s, c, u2.at[c, 1, 1:17], u2.at[c, 4, 1:17], u2.at[c, 0, 1:17], u2.at[c, 5, 1:17], hh_s, hh_r
    )
    for planes in ((0, 3), (1, 2)):
        convolve_pair(
            lambda p, b: u1[p, pl.ds(b, 16)].reshape(256, 512),
            lambda k: f1[k].reshape(512, 128),
            planes,
            acc,
        )
        for index, p in enumerate(planes):
            pre = plane_of(acc, index) + b1[...]
            slope[p] = slope_of(pre)
            u2[c, p + 1, 1:17] = (pre * jax.nn.sigmoid(pre)).astype(BF).reshape(16, 16, 128)
        if planes == (0, 3):
            hidden_halo.start()
    hidden_halo.wait_recv()
    channels = ChanGather(lambda cb: u2.at[cb, :, 1:17], s, y, core, hy_s, hy_r, hc_s, hc_r)
    channels.start_own()
    for d in RING:
        second.forward(d)
    channels.forward()
    channels.finish()
    second.wait_second()
    save_u2 = pltpu.make_async_copy(u2, u2_out, loc.at[5])
    save_w2 = pltpu.make_async_copy(f2, w2_out, loc.at[6])
    save_u2.start()
    save_w2.start()

    for planes in ((0, 3), (1, 2)):
        convolve_pair(
            lambda p, b: jnp.concatenate([u2[q, p, pl.ds(b, 16)].reshape(256, 128) for q in range(8)], axis=1),
            lambda k: f2[k].reshape(1024, 128),
            planes,
            acc,
        )
        for index, p in enumerate(planes):
            pre = plane_of(acc, index) + b2[...]
            feat[p] = (pre * jax.nn.sigmoid(pre)).astype(BF).reshape(16, 16, 128)
            adjoint = cot[p].reshape(256, 128).astype(F32) * slope_of(pre)
            stack_shifts(adjoint, p, stacked, 0, 0, flipped)
    halo.wait_send()
    hidden_halo.wait_send()
    rows.wait_send()
    channels.wait_send()
    first.wait_send()
    second.wait_send()
    for copy in (save_u1, save_w1, save_u2, save_w2):
        copy.wait()


class Scatter:
    def __init__(self, terms, got1, mid, got2, total, out, x, z, c, sems, flip):
        self.terms, self.got1, self.mid, self.got2 = terms, got1, mid, got2
        self.total, self.out = total, out
        self.x, self.z, self.c, self.flip = x, z, c, flip
        self.s1, self.r1, self.s2, self.r2 = sems

    def by_axis(self, j, act):
        x_first = lax.rem(j + self.flip, 2) == 0

        @pl.when(x_first)
        def _():
            act(True)

        @pl.when(jnp.logical_not(x_first))
        def _():
            act(False)

    def target(self, along_x, d):
        tx = lax.rem(self.x + d, 4) if along_x else self.x
        tz = self.z if along_x else lax.rem(self.z + d, 4)
        return tx, tz

    def stage1(self, j, d, x_first):
        tx, tz = self.target(x_first, d)
        src = self.terms.at[pl.ds(3 * j, 3), tx] if x_first else self.terms.at[pl.ds(3 * j, 3), :, tz]
        return send(
            src, self.got1.at[j, d - 1], self.s1.at[j, d - 1], self.r1.at[j, d - 1], (tx * 4 + tz, self.c)
        )

    def stage2(self, j, d, x_first):
        tx, tz = self.target(not x_first, d)
        src = self.mid.at[j, :, tz] if x_first else self.mid.at[j, :, tx]
        return send(
            src, self.got2.at[j, d - 1], self.s2.at[j, d - 1], self.r2.at[j, d - 1], (tx * 4 + tz, self.c)
        )

    def start1(self, j):
        def act(x_first):
            for d in RING:
                self.stage1(j, d, x_first).start()

        self.by_axis(j, act)

    def start2(self, j):
        def act(x_first):
            for d in RING:
                self.stage1(j, d, x_first).wait_recv()
            own = self.terms[pl.ds(3 * j, 3), self.x] if x_first else self.terms[pl.ds(3 * j, 3), :, self.z]
            value = own.astype(F32)
            for d in range(3):
                value = value + self.got1[j, d].astype(F32)
            self.total[...] = value
            self.mid[j] = value.astype(BF)
            self.out[pl.ds(3 * j, 3)] = self.total[:, self.z] if x_first else self.total[:, self.x]
            for d in RING:
                self.stage2(j, d, x_first).start()

        self.by_axis(j, act)

    def finish(self, j):
        def act(x_first):
            for d in RING:
                self.stage2(j, d, x_first).wait_recv()
            value = self.out[pl.ds(3 * j, 3)]
            for d in range(3):
                value = value + self.got2[j, d].astype(F32)
            self.out[pl.ds(3 * j, 3)] = value
            for d in RING:
                self.stage1(j, d, x_first).wait_send()
                self.stage2(j, d, x_first).wait_send()

        self.by_axis(j, act)


def every_chunk(act):
    def step(j, _):
        act(j)
        return 0

    lax.fori_loop(0, 9, step, 0)


def back_columns(stacked, load_w):
    total = None
    for a in range(3):
        rows = jnp.concatenate(
            [stacked[2 - a : 6 - a, 2 - b : 18 - b].reshape(1024, 384) for b in range(3)], axis=1
        )
        filters = jnp.concatenate([load_w(9 * a + k) for k in range(9)], axis=1)
        term = lax.dot_general(rows, filters, (((1,), (1,)), ((), ())), preferred_element_type=F32)
        total = term if total is None else total + term
    return total


def backward_kernel(
    stacked_in, flipped2, slope, u1_in, u2, w1_in, w2_in,
    grad_in, grad1, grad2,
    u1, f1, f2, adj2, adj1, flipped1,
    terms2, got2a, mid2, got2b, total2,
    terms1, got1a, mid1, got1b, total1,
    hid_own, hid_bf, hid_sib, hid_sum, hid_got,
    inp_own, inp_bf, inp_sib, inp_sum, inp_got,
    g2s1, g2r1, g2s2, g2r2, g1s1, g1r1, g1s2, g1r2,
    h2s, h2r, h1s, h1r, hss, hsr, hys, hyr, iss, isr, iys, iyr, loc,
):
    s, c, x, z, y, core = place()
    loads = [
        pltpu.make_async_copy(stacked_in, adj2.at[1:5, 1:17], loc.at[0]),
        pltpu.make_async_copy(w2_in, f2, loc.at[1]),
        pltpu.make_async_copy(u1_in, u1, loc.at[2]),
        pltpu.make_async_copy(w1_in, f1, loc.at[3]),
    ]
    for copy in loads:
        copy.start()
    for field in (adj2, adj1):
        for plane in (0, 5):
            field[plane] = jnp.zeros((18, 16, 384), BF)
        for row in (0, 17):
            field[1:5, row] = jnp.zeros((4, 16, 384), BF)
    greet(s, c, x, z)
    sibling = (s, y * 2 + 1 - core)

    halo2 = Halo(
        s, c, stacked_in.at[0], stacked_in.at[3], adj2.at[0, 1:17], adj2.at[5, 1:17], h2s, h2r
    )
    halo2.start()
    scatter2 = Scatter(
        terms2, got2a, mid2, got2b, total2, grad2, x, z, c, (g2s1, g2r1, g2s2, g2r2), 0
    )
    scatter1 = Scatter(
        terms1, got1a, mid1, got1b, total1, grad1, x, z, c, (g1s1, g1r1, g1s2, g1r2), 1
    )

    def second_chunk(j):
        a, b = lax.div(j, 3), lax.rem(j, 3)

        def block(n, _):
            fields = [u2[2 * n + q, pl.ds(a, 4), pl.ds(b, 16)].reshape(1024, 128) for q in range(2)]
            turned = dot(flipped2[...], jnp.concatenate(fields, axis=1)).T.astype(BF)
            for k in range(3):
                terms2[3 * j + k, n] = turned[:, k * 128 : (k + 1) * 128].reshape(4, 64, 128)
            return 0

        lax.fori_loop(0, 4, block, 0)
        scatter2.start1(j)

    every_chunk(second_chunk)
    for copy in loads:
        copy.wait()
    halo2.wait_recv()

    def hidden_to_sibling(n):
        return send(hid_bf.at[n, 1 - core], hid_sib.at[n], hss.at[n], hsr.at[n], sibling)

    def hidden_columns(n, _):
        value = back_columns(adj2, lambda k: f2[k, n].reshape(256, 128))
        low, high = value[:, :128], value[:, 128:]
        hid_bf[n, 0] = low.astype(BF)
        hid_bf[n, 1] = high.astype(BF)
        hid_own[n] = jnp.where(core == 0, low, high)
        hidden_to_sibling(n).start()
        return 0

    lax.fori_loop(0, 4, hidden_columns, 0)

    def hidden_to_y(d):
        n = lax.rem(y + d, 4)
        return send(hid_sum.at[n], hid_got.at[d - 1], hys.at[d - 1], hyr.at[d - 1], (s, n * 2 + core))

    for d in (1, 3, 2, 0):
        n = lax.rem(y + d, 4)
        hidden_to_sibling(n).wait_recv()
        pair = hid_own[n] + hid_sib[n].astype(F32)
        if d:
            hid_sum[n] = pair.astype(BF)
            hidden_to_y(d).start()
        else:
            hid_own[n] = pair
    for d in RING:
        hidden_to_y(d).wait_recv()
    for p in range(4):
        rows = slice(p * 256, (p + 1) * 256)
        value = hid_own[y, rows]
        for d in range(3):
            value = value + hid_got[d, rows].astype(F32)
        stack_shifts(value * slope[p], p, adj1, 1, 1, flipped1)
    halo1 = Halo(
        s, c, adj1.at[1, 1:17], adj1.at[4, 1:17], adj1.at[0, 1:17], adj1.at[5, 1:17], h1s, h1r
    )
    halo1.start()

    def first_chunk(j):
        a, b = lax.div(j, 3), lax.rem(j, 3)
        for n in range(2):
            field = u1[pl.ds(a, 4), pl.ds(b, 16), :, n * 256 : (n + 1) * 256].reshape(1024, 256)
            turned = dot(flipped1[...], field).T.astype(BF)
            for k in range(3):
                terms1[3 * j + k, 2 * n : 2 * n + 2] = turned[:, k * 128 : (k + 1) * 128].reshape(2, 4, 32, 128)
        scatter1.start1(j)

    every_chunk(first_chunk)
    halo1.wait_recv()
    for n in range(2):
        value = back_columns(adj1, lambda k: f1[k, 2 * n : 2 * n + 2].reshape(256, 128))
        value = value.reshape(4, 4, 2, 2, 16, 256)
        columns = slice(n * 256, (n + 1) * 256)
        inp_own[:, :, :, :, :, columns] = value
        inp_bf[:, :, :, :, :, columns] = value.astype(BF)
    to_sibling = send(inp_bf.at[:, :, 1 - core], inp_sib, iss.at[0], isr.at[0], sibling)
    to_sibling.start()

    def input_to_y(d):
        n = lax.rem(y + d, 4)
        return send(inp_sum.at[n], inp_got.at[d - 1], iys.at[d - 1], iyr.at[d - 1], (s, n * 2 + core))

    to_sibling.wait_recv()
    for d in (1, 3, 2, 0):
        n = lax.rem(y + d, 4)
        pair = inp_own[:, n, core] + inp_sib[:, n].astype(F32)
        if d:
            inp_sum[n] = pair.astype(BF)
            input_to_y(d).start()
        else:
            grad_in[...] = pair
    every_chunk(scatter2.start2)
    for d in RING:
        input_to_y(d).wait_recv()
    value = grad_in[...]
    for d in range(3):
        value = value + inp_got[d].astype(F32)
    grad_in[...] = value
    every_chunk(scatter1.start2)
    every_chunk(scatter2.finish)
    every_chunk(scatter1.finish)

    halo2.wait_send()
    halo1.wait_send()
    to_sibling.wait_send()
    for n in range(4):
        hidden_to_sibling(n).wait_send()
    for d in RING:
        hidden_to_y(d).wait_send()
        input_to_y(d).wait_send()


def vmem(count):
    return [pl.BlockSpec(memory_space=pltpu.VMEM)] * count


def anywhere(count):
    return [pl.BlockSpec(memory_space=pl.ANY)] * count


def dma(*shape):
    return pltpu.SemaphoreType.DMA(shape)


def local(volume, w_first, b_first, w_second, b_second, cotangent):
    shape = jax.ShapeDtypeStruct
    flops = 2 * 1024 * 27 * 128 * 1536
    features, stacked, flipped, slope, u1, u2, f1, f2 = pl.pallas_call(
        forward_kernel,
        name="forward",
        out_shape=(
            shape((4, 16, 16, 128), BF),
            shape((4, 16, 16, 384), BF),
            shape((384, 1024), BF),
            shape((4, 256, 128), F32),
            shape((6, 18, 16, 512), BF),
            shape((8, 6, 18, 16, 128), BF),
            shape((27, 4, 4, 32, 128), BF),
            shape((27, 4, 4, 64, 128), BF),
        ),
        in_specs=vmem(1) + anywhere(1) + vmem(1) + anywhere(1) + vmem(2),
        out_specs=tuple(vmem(4) + anywhere(4)),
        scratch_shapes=[
            pltpu.VMEM((6, 18, 16, 512), BF),
            pltpu.VMEM((8, 6, 18, 16, 128), BF),
            pltpu.VMEM((27, 4, 4, 32, 128), BF),
            pltpu.VMEM((27, 4, 4, 64, 128), BF),
            pltpu.VMEM((512, 384), F32),
            dma(2, 16), dma(2, 16), dma(2, 16), dma(2, 16),
            dma(2), dma(2), dma(2), dma(2),
            dma(4), dma(4), dma(4), dma(4), dma(4), dma(4), dma(4), dma(4),
            dma(8),
        ],
        compiler_params=pltpu.CompilerParams(
            collective_id=0, has_side_effects=True, vmem_limit_bytes=VMEM_BYTES
        ),
        cost_estimate=pl.CostEstimate(flops=flops, bytes_accessed=40_000_000, transcendentals=600_000),
    )(volume, w_first, b_first.reshape(1, 128), w_second, b_second.reshape(1, 128), cotangent)
    grad_input, grad_first, grad_second = pl.pallas_call(
        backward_kernel,
        name="backward",
        out_shape=(
            shape((4, 2, 16, 512), F32),
            shape((27, 32, 128), F32),
            shape((27, 64, 128), F32),
        ),
        in_specs=vmem(3) + anywhere(1) + vmem(1) + anywhere(2),
        out_specs=tuple(vmem(3)),
        scratch_shapes=[
            pltpu.VMEM((6, 18, 16, 512), BF),
            pltpu.VMEM((27, 4, 4, 32, 128), BF),
            pltpu.VMEM((27, 4, 4, 64, 128), BF),
            pltpu.VMEM((6, 18, 16, 384), BF),
            pltpu.VMEM((6, 18, 16, 384), BF),
            pltpu.VMEM((384, 1024), BF),
            pltpu.VMEM((27, 4, 4, 64, 128), BF),
            pltpu.VMEM((9, 3, 3, 4, 64, 128), BF),
            pltpu.VMEM((9, 3, 4, 64, 128), BF),
            pltpu.VMEM((9, 3, 3, 64, 128), BF),
            pltpu.VMEM((3, 4, 64, 128), F32),
            pltpu.VMEM((27, 4, 4, 32, 128), BF),
            pltpu.VMEM((9, 3, 3, 4, 32, 128), BF),
            pltpu.VMEM((9, 3, 4, 32, 128), BF),
            pltpu.VMEM((9, 3, 3, 32, 128), BF),
            pltpu.VMEM((3, 4, 32, 128), F32),
            pltpu.VMEM((4, 1024, 128), F32),
            pltpu.VMEM((4, 2, 1024, 128), BF),
            pltpu.VMEM((4, 1024, 128), BF),
            pltpu.VMEM((4, 1024, 128), BF),
            pltpu.VMEM((3, 1024, 128), BF),
            pltpu.VMEM((4, 4, 2, 2, 16, 512), F32),
            pltpu.VMEM((4, 4, 2, 2, 16, 512), BF),
            pltpu.VMEM((4, 4, 2, 16, 512), BF),
            pltpu.VMEM((4, 4, 2, 16, 512), BF),
            pltpu.VMEM((3, 4, 2, 16, 512), BF),
            dma(9, 3), dma(9, 3), dma(9, 3), dma(9, 3),
            dma(9, 3), dma(9, 3), dma(9, 3), dma(9, 3),
            dma(2), dma(2), dma(2), dma(2),
            dma(4), dma(4), dma(3), dma(3),
            dma(1), dma(1), dma(3), dma(3),
            dma(4),
        ],
        compiler_params=pltpu.CompilerParams(
            collective_id=1, has_side_effects=True, vmem_limit_bytes=VMEM_BYTES
        ),
        cost_estimate=pl.CostEstimate(flops=2 * flops, bytes_accessed=40_000_000, transcendentals=0),
    )(stacked, flipped, slope, u1, u2, f1, f2)
    return (features, grad_input, grad_first, grad_second)


def solution(mesh):
    return jax.shard_map(
        local,
        mesh=mesh,
        in_specs=(
            P("space", "chan", None, None),
            P(None, "space", "chan"),
            P("chan"),
            P(None, "space", "chan"),
            P("chan"),
            P("space", None, None, "chan"),
        ),
        out_specs=(
            P("space", None, None, "chan"),
            P("space", "chan", None, None),
            P(None, "space", "chan"),
            P(None, "space", "chan"),
        ),
        check_vma=False,
    )
```

time: 768 us -> 204 us (0.27)
  waiting for transfers between devices: 346 us -> 0 us
  matrix products: 277 us -> 0 us
  Pallas kernels: 0 us -> 195 us
  local copies, waits for them, and re-layouts: 93.9 us -> 6.35 us
  starting transfers between devices: 19.4 us -> 0 us
  between operations: 16.7 us -> 0.67 us
  other arithmetic: 8.64 us -> 0 us
    dot_general x162 -> x0, matrix products: 277 us -> none  [the longest x54 172 us: convolve_back(): jnp.dot(sliced, weights[offset].T, preferred_element_type=jnp.float32)]
    reduce_scatter x3 -> x0, waiting for transfers between devices: 199 us -> none  [the longest x1 104 us: local(): lax.psum_scatter(parts_second, 'space', scatter_dimension=1, tiled=True)]
    pallas_call x0 -> x2, Pallas kernels: none -> 195 us  [the longest x1 104 us: local(): pl.pallas_call(forward_kernel, name='forward', out_shape=(shape((4, 16, 1...]
    all_gather x4 -> x0, waiting for transfers between devices: 130 us -> none  [the longest x1 42 us: local(): lax.all_gather(w_second, 'space', axis=1, tiled=True)]
    slice x16 -> x0, local copies, waits for them, and re-layouts: 78.2 us -> none  [the longest x4 38.1 us: convolve(): padded[a:a + span_x, b:b + span_y, c:c + span_z]]
    ppermute x8 -> x0, starting transfers between devices: 18.7 us -> none  [the longest x4 13.4 us: with_halo(): lax.ppermute(tail, axis, [(i, (i + 1) % count) for i in range(ends)])]
    ppermute x8 -> x0, waiting for transfers between devices: 15.8 us -> none  [the longest x4 10.6 us: with_halo(): lax.ppermute(head, axis, [((i + 1) % count, i) for i in range(ends)])]
  transfers between devices with their start and end apart: 16 -> 0, of which waited for: 12 -> 0; matrix products, arithmetic and copies ran while one was open for 20% -> 0% of each run, Pallas kernels for 0% -> 0%
where the time goes in v1:
time: 204 us; the launch traced here: 203 us
  Pallas kernels  195 us (96%)
  local copies, waits for them, and re-layouts  6.35 us (3%)
    pallas_call x1, Pallas kernels, local(): pl.pallas_call(forward_kernel, name='forward', out_shape=(shape((4, 16, 1...  104 us
    pallas_call x1, Pallas kernels, local(): pl.pallas_call(backward_kernel, name='backward', out_shape=(shape((4, 2,...  91.7 us
    unnamed x6, local copies, waits for them, and re-layouts  6.35 us

profile of v1, /device:TPU:0, one launch (start us, length us, event | category | flops | bytes accessed | tf_op | source)
XLA Modules:
  0.0 202.5 jit_solution(7612453118826685890)
XLA Ops:
  0.6 103.8 %forward.1 = (bf16[4,16,16,128]{3,2,1,0:T(8,128)(2,1)}, bf16[4,16,16,384]{3,2,1,0:T(8,128)(2,1)}, bf16[384,1024]{1,0:T(8,128)(2,1)}, f32[4,256,128]{2,1,0:T(8,12...) custom-call(bf16[4,2,16,512]{3,2,1,0:T(8,128)(2,1)} %vol.1, ...), custom_call_target="tpu_custom_call" | custom-call | flops 10871635968 | bytes 40000000 | tf_op jit(solution)/shard_map/forward/pallas_call | solution.py:618
  104.4 0.0 copy-start
  104.4 91.7 %backward.1 = (f32[4,2,16,512]{3,2,1,0:T(8,128)}, f32[27,32,128]{2,1,0:T(8,128)}, f32[27,64,128]{2,1,0:T(8,128)}) custom-call(bf16[4,16,16,384]{3,2,1,0:T(8,128)(2,1)} %get-tuple-element.16.stacked_in, bf16[384,1024]{1,0:T(8,128)(2,1)} %get-tuple-element.17.flipped2, f32[4,256,128]{2,1,0:T(8,128)} %get-tuple-element.18.slope, ...), custom_call_target="tpu_custom_call" | custom-call | flops 21743271936 | bytes 40000000 | tf_op jit(solution)/shard_map/backward/pallas_call | solution.py:649
  196.2 0.0 copy-done
  196.2 0.7 copy.14
  196.9 1.7 copy.15
  198.5 1.8 copy.16
  200.3 2.2 %copy.17 = f32[27,64,128]{2,1,0:T(8,128)} copy(f32[27,64,128]{2,1,0:T(8,128)} %get-tuple-element.33) | data formatting | bytes 1769472
Async XLA Ops:
  104.4 91.7 %copy-start = (bf16[4,16,16,128]{3,2,1,0:T(8,128)(2,1)S(1)}, bf16[4,16,16,128]{3,2,1,0:T(8,128)(2,1)}, u32[]{:S(2)}) copy-start(bf16[4,16,16,128]{3,2,1,0:T(8,128)(2,1)} %get-tuple-element.30) | copy-start | bytes 786436

commit v2 on v1

--- a/solution.py
+++ b/solution.py
@@ -13,6 +13,7 @@
 VMEM_BYTES = 63 * 1024 * 1024
 RING = (1, 3, 2)
 HALVES = ((0, 14), (14, 13))
+THIRDS = (((0, 5), (5, 4)), ((9, 4), (13, 5)), ((18, 5), (23, 4)))
 
 
 def place():
@@ -81,80 +82,90 @@
         pl.when(self.s < 15)(self.up.wait_send)
 
 
+HOPS = ((1, 0, 0), (3, 0, 0), (1, 1, 1), (3, 3, 2))
+
+
 class Gather:
-    def __init__(self, own, full, x, z, c, send_sem, recv_sem):
-        self.own, self.full, self.x, self.z, self.c = own, full, x, z, c
+    def __init__(self, own, full, x, z, c, send_sem, recv_sem, halves):
+        self.own, self.full, self.x, self.z, self.c, self.halves = own, full, x, z, c, halves
         self.send_sem, self.recv_sem = send_sem, recv_sem
 
-    def copy(self, half, first, second, source_own, stage):
-        k0, nk = HALVES[half]
-        back1, back2 = (first, second)
-        if stage == 1:
-            o1, o2 = 0, 0
-        else:
-            o1, o2 = back1, 0
-        if half == 0:
-            ox, oz = lax.rem(self.x + 4 - o1, 4), self.z
-            tx = lax.rem(self.x + back1, 4) if stage == 1 else self.x
-            tz = self.z if stage == 1 else lax.rem(self.z + back2, 4)
-        else:
-            ox, oz = self.x, lax.rem(self.z + 4 - o1, 4)
-            tz = lax.rem(self.z + back1, 4) if stage == 1 else self.z
-            tx = self.x if stage == 1 else lax.rem(self.x + back2, 4)
-        dst = self.full.at[pl.ds(k0, nk), ox, oz]
-        src = self.own.at[pl.ds(k0, nk)] if source_own else dst
-        index = first * 4 + second
+    def span(self, half, part):
+        k0, nk = self.halves[half]
+        cut = (nk + 1) // 2
+        return ((k0, nk), (k0, cut), (k0 + cut, nk - cut))[part]
+
+    def region(self, half, first, second, part):
+        ox = lax.rem(self.x + 4 - (second if half else first), 4)
+        oz = lax.rem(self.z + 4 - (first if half else second), 4)
+        k0, nk = self.span(half, part)
+        return self.full.at[pl.ds(k0, nk), ox, oz]
+
+    def copy(self, half, row, hop):
+        step, behind_by, part = HOPS[hop]
+        first, second = (behind_by, 0) if row == 0 else (row - 1, behind_by)
+        dst = self.region(half, first, second, part)
+        k0, nk = self.span(half, part)
+        src = self.own.at[pl.ds(k0, nk)] if first == 0 and second == 0 else dst
+        along_x = (row == 0) == (half == 0)
+        tx = lax.rem(self.x + step, 4) if along_x else self.x
+        tz = self.z if along_x else lax.rem(self.z + step, 4)
         return send(
-            src,
-            dst,
-            self.send_sem.at[half, index],
-            self.recv_sem.at[half, index],
-            (tx * 4 + tz, self.c),
+            src, dst, self.send_sem.at[half, row, hop], self.recv_sem.at[half, row, hop], (tx * 4 + tz, self.c)
         )
 
-    def arrived(self, half, first, second):
-        k0, nk = HALVES[half]
-        if half == 0:
-            ox, oz = lax.rem(self.x + 4 - first, 4), lax.rem(self.z + 4 - second, 4)
-        else:
-            oz, ox = lax.rem(self.z + 4 - first, 4), lax.rem(self.x + 4 - second, 4)
-        region = self.full.at[pl.ds(k0, nk), ox, oz]
-        index = first * 4 + second
+    def arrived(self, half, row, hop):
+        step, behind_by, part = HOPS[hop]
+        distance = (step + behind_by) % 4
+        first, second = (distance, 0) if row == 0 else (row - 1, distance)
+        region = self.region(half, first, second, part)
         send(
             region,
             region,
-            self.send_sem.at[half, index],
-            self.recv_sem.at[half, index],
+            self.send_sem.at[half, row, hop],
+            self.recv_sem.at[half, row, hop],
             (lax.rem(self.x + 1, 4) * 4 + self.z, self.c),
         ).wait_recv()
 
+    def start_row(self, half, row):
+        self.copy(half, row, 0).start()
+        self.copy(half, row, 1).start()
+
     def start_own(self):
-        for d in RING:
+        for row in (0, 1):
             for half in (0, 1):
-                self.copy(half, d, 0, True, 1).start()
-        for d in RING:
+                self.start_row(half, row)
+
+    def near(self):
+        for hop, d in ((0, 1), (1, 3)):
             for half in (0, 1):
-                self.copy(half, 0, d, True, 2).start()
-
-    def forward(self, d):
+                self.arrived(half, 0, hop)
+                self.copy(half, 0, hop + 2).start()
+                self.start_row(half, 1 + d)
+
+    def relay(self, d):
+        for hop in (0, 1):
+            for half in (0, 1):
+                self.arrived(half, 1 + d, hop)
+                self.copy(half, 1 + d, hop + 2).start()
+
+    def far(self):
         for half in (0, 1):
-            self.arrived(half, d, 0)
-            for e in RING:
-                self.copy(half, d, e, False, 2).start()
-
-    def wait_second(self):
-        for d in range(4):
-            for e in RING:
-                for half in (0, 1):
-                    self.arrived(half, d, e)
+            self.arrived(half, 0, 2)
+            self.arrived(half, 0, 3)
+            self.start_row(half, 3)
+
+    def finish(self):
+        for d in (0, 1, 3, 2):
+            for half in (0, 1):
+                self.arrived(half, 1 + d, 2)
+                self.arrived(half, 1 + d, 3)
 
     def wait_send(self):
         for half in (0, 1):
-            for d in RING:
-                self.copy(half, d, 0, True, 1).wait_send()
-            for d in range(4):
-                for e in RING:
-                    self.copy(half, d, e, d == 0, 2).wait_send()
+            for row in range(5):
+                for hop in range(4):
+                    self.copy(half, row, hop).wait_send()
 
 
 class ChanGather:
@@ -243,6 +254,18 @@
     lax.fori_loop(0, 9, step, 0)
 
 
+def convolve_second(field, filters, acc, a):
+    def step(b, _):
+        rows = jnp.concatenate(
+            [field[q, a : a + 4, pl.ds(b, 16)].reshape(1024, 128) for q in range(8)], axis=1
+        )
+        columns = [filters[9 * a + 3 * b + k].reshape(1024, 128) for k in range(3)]
+        acc[...] += dot(rows, jnp.concatenate(columns, axis=1))
+        return 0
+
+    lax.fori_loop(0, 3, step, 0)
+
+
 def plane_of(acc, index):
     rows = slice(index * 256, (index + 1) * 256)
     return behind(acc[rows, 0:128]) + acc[rows, 128:256] + ahead(acc[rows, 256:384])
@@ -251,7 +274,7 @@
 def forward_kernel(
     vol, w1, b1, w2, b2, cot,
     feat, stacked, flipped, slope, u1_out, u2_out, w1_out, w2_out,
-    u1, u2, f1, f2, acc,
+    u1, u2, f1, f2, acc, acc2,
     ag1_s, ag1_r, ag2_s, ag2_r, halo_s, halo_r, hh_s, hh_r, y_s, y_r, c_s, c_r, hy_s, hy_r, hc_s, hc_r, loc,
 ):
     s, c, x, z, y, core = place()
@@ -278,8 +301,8 @@
         copy.start()
     greet(s, c, x, z)
 
-    first = Gather(w1, f1, x, z, c, ag1_s, ag1_r)
-    second = Gather(w2, f2, x, z, c, ag2_s, ag2_r)
+    first = Gather(w1, f1, x, z, c, ag1_s, ag1_r, HALVES)
+    second = [Gather(w2, f2, x, z, c, ag2_s.at[i], ag2_r.at[i], THIRDS[i]) for i in range(3)]
     halo = Halo(
         s, c, vol.at[0], vol.at[3],
         u1.at[0, pl.ds(1 + 2 * c, 2)], u1.at[5, pl.ds(1 + 2 * c, 2)], halo_s, halo_r,
@@ -290,14 +313,19 @@
     locals_[0].wait()
     halo.wait_recv()
     rows.start_own()
-    for d in RING:
-        first.forward(d)
-    second.start_own()
+    first.near()
+    first.relay(0)
+    first.far()
     rows.forward()
+    first.relay(1)
+    first.relay(3)
+    first.relay(2)
+    second[0].start_own()
+    second[1].start_own()
     rows.finish()
     locals_[1].wait()
     locals_[2].wait()
-    first.wait_second()
+    first.finish()
     save_u1 = pltpu.make_async_copy(u1, u1_out, loc.at[3])
     save_w1 = pltpu.make_async_copy(f1, w1_out, loc.at[4])
     save_u1.start()
@@ -319,47 +347,65 @@
             u2[c, p + 1, 1:17] = (pre * jax.nn.sigmoid(pre)).astype(BF).reshape(16, 16, 128)
         if planes == (0, 3):
             hidden_halo.start()
+            second[0].near()
     hidden_halo.wait_recv()
     channels = ChanGather(lambda cb: u2.at[cb, :, 1:17], s, y, core, hy_s, hy_r, hc_s, hc_r)
     channels.start_own()
-    for d in RING:
-        second.forward(d)
+    second[0].relay(0)
+    second[0].far()
+    second[1].near()
+    second[2].start_own()
+    second[0].relay(1)
+    second[0].relay(3)
+    second[0].relay(2)
+    second[1].relay(0)
     channels.forward()
+    second[1].far()
+    second[2].near()
+    second[1].relay(1)
+    second[1].relay(3)
     channels.finish()
-    second.wait_second()
     save_u2 = pltpu.make_async_copy(u2, u2_out, loc.at[5])
+    save_u2.start()
+    second[1].relay(2)
+    second[0].finish()
+    acc2[...] = jnp.zeros_like(acc2)
+    for a in range(3):
+        convolve_second(u2, f2, acc2, a)
+        if a == 0:
+            second[2].relay(0)
+            second[2].far()
+            second[2].relay(1)
+            second[2].relay(3)
+            second[2].relay(2)
+        if a < 2:
+            second[a + 1].finish()
     save_w2 = pltpu.make_async_copy(f2, w2_out, loc.at[6])
-    save_u2.start()
     save_w2.start()
-
-    for planes in ((0, 3), (1, 2)):
-        convolve_pair(
-            lambda p, b: jnp.concatenate([u2[q, p, pl.ds(b, 16)].reshape(256, 128) for q in range(8)], axis=1),
-            lambda k: f2[k].reshape(1024, 128),
-            planes,
-            acc,
-        )
-        for index, p in enumerate(planes):
-            pre = plane_of(acc, index) + b2[...]
-            feat[p] = (pre * jax.nn.sigmoid(pre)).astype(BF).reshape(16, 16, 128)
-            adjoint = cot[p].reshape(256, 128).astype(F32) * slope_of(pre)
-            stack_shifts(adjoint, p, stacked, 0, 0, flipped)
+    for p in range(4):
+        pre = plane_of(acc2, p) + b2[...]
+        feat[p] = (pre * jax.nn.sigmoid(pre)).astype(BF).reshape(16, 16, 128)
+        adjoint = cot[p].reshape(256, 128).astype(F32) * slope_of(pre)
+        stack_shifts(adjoint, p, stacked, 0, 0, flipped)
     halo.wait_send()
     hidden_halo.wait_send()
     rows.wait_send()
     channels.wait_send()
     first.wait_send()
-    second.wait_send()
+    for part in second:
+        part.wait_send()
     for copy in (save_u1, save_w1, save_u2, save_w2):
         copy.wait()
 
 
 class Scatter:
-    def __init__(self, terms, got1, mid, got2, total, out, x, z, c, sems, flip):
-        self.terms, self.got1, self.mid, self.got2 = terms, got1, mid, got2
+    def __init__(self, terms, far1, near1, mid, far2, near2, total, out, x, z, c, sems, flip):
+        self.terms, self.far1, self.near1 = terms, far1, near1
+        self.mid, self.far2, self.near2 = mid, far2, near2
         self.total, self.out = total, out
         self.x, self.z, self.c, self.flip = x, z, c, flip
         self.s1, self.r1, self.s2, self.r2 = sems
+        self.rows = out.shape[1]
 
     def by_axis(self, j, act):
         x_first = lax.rem(j + self.flip, 2) == 0
@@ -375,66 +421,101 @@
     def target(self, along_x, d):
         tx = lax.rem(self.x + d, 4) if along_x else self.x
         tz = self.z if along_x else lax.rem(self.z + d, 4)
-        return tx, tz
-
-    def stage1(self, j, d, x_first):
-        tx, tz = self.target(x_first, d)
-        src = self.terms.at[pl.ds(3 * j, 3), tx] if x_first else self.terms.at[pl.ds(3 * j, 3), :, tz]
-        return send(
-            src, self.got1.at[j, d - 1], self.s1.at[j, d - 1], self.r1.at[j, d - 1], (tx * 4 + tz, self.c)
+        return tx * 4 + tz, self.c
+
+    def block1(self, j, x_first, d, part=None):
+        offsets = pl.ds(3 * j, 3)
+        if x_first:
+            lead = (offsets, lax.rem(self.x + d, 4))
+            return lead if part is None else lead + (slice(2 * part, 2 * part + 2),)
+        at = lax.rem(self.z + d, 4)
+        return (offsets, slice(None) if part is None else slice(2 * part, 2 * part + 2), at)
+
+    def block2(self, j, x_first, d, part=None):
+        at = lax.rem((self.z if x_first else self.x) + d, 4)
+        half = self.rows // 2
+        lead = (j, slice(None), at)
+        return lead if part is None else lead + (slice(half * part, half * (part + 1)),)
+
+    def far(self, stage, j, x_first, way):
+        src, dst = (
+            (self.terms.at[self.block1(j, x_first, 2, way)], self.far1)
+            if stage == 1
+            else (self.mid.at[self.block2(j, x_first, 2, way)], self.far2)
         )
-
-    def stage2(self, j, d, x_first):
-        tx, tz = self.target(not x_first, d)
-        src = self.mid.at[j, :, tz] if x_first else self.mid.at[j, :, tx]
-        return send(
-            src, self.got2.at[j, d - 1], self.s2.at[j, d - 1], self.r2.at[j, d - 1], (tx * 4 + tz, self.c)
+        s, r = (self.s1, self.r1) if stage == 1 else (self.s2, self.r2)
+        to = self.target(x_first == (stage == 1), (1, 3)[way])
+        return send(src, dst.at[j, way], s.at[j, way], r.at[j, way], to)
+
+    def near(self, stage, j, x_first, way):
+        step = (1, 3)[way]
+        src, dst = (
+            (self.terms.at[self.block1(j, x_first, step)], self.near1)
+            if stage == 1
+            else (self.mid.at[self.block2(j, x_first, step)], self.near2)
         )
+        s, r = (self.s1, self.r1) if stage == 1 else (self.s2, self.r2)
+        to = self.target(x_first == (stage == 1), step)
+        return send(src, dst.at[j, way], s.at[j, 2 + way], r.at[j, 2 + way], to)
+
+    def pass_on(self, stage, j, x_first):
+        for way, step in ((0, 1), (1, 3)):
+            self.far(stage, j, x_first, way).wait_recv()
+            if stage == 1:
+                field, got, where = self.terms, self.far1, self.block1(j, x_first, step, way)
+            else:
+                field, got, where = self.mid, self.far2, self.block2(j, x_first, step, way)
+            field[where] = (field[where].astype(F32) + got[j, way].astype(F32)).astype(BF)
+            self.near(stage, j, x_first, way).start()
 
     def start1(self, j):
         def act(x_first):
-            for d in RING:
-                self.stage1(j, d, x_first).start()
+            self.far(1, j, x_first, 0).start()
+            self.far(1, j, x_first, 1).start()
 
         self.by_axis(j, act)
+
+    def relay1(self, j):
+        self.by_axis(j, lambda x_first: self.pass_on(1, j, x_first))
 
     def start2(self, j):
         def act(x_first):
-            for d in RING:
-                self.stage1(j, d, x_first).wait_recv()
-            own = self.terms[pl.ds(3 * j, 3), self.x] if x_first else self.terms[pl.ds(3 * j, 3), :, self.z]
-            value = own.astype(F32)
-            for d in range(3):
-                value = value + self.got1[j, d].astype(F32)
+            value = self.terms[self.block1(j, x_first, 0)].astype(F32)
+            for way in (0, 1):
+                self.near(1, j, x_first, way).wait_recv()
+                value = value + self.near1[j, way].astype(F32)
             self.total[...] = value
             self.mid[j] = value.astype(BF)
+            self.far(2, j, x_first, 0).start()
+            self.far(2, j, x_first, 1).start()
             self.out[pl.ds(3 * j, 3)] = self.total[:, self.z] if x_first else self.total[:, self.x]
-            for d in RING:
-                self.stage2(j, d, x_first).start()
 
         self.by_axis(j, act)
+
+    def relay2(self, j):
+        self.by_axis(j, lambda x_first: self.pass_on(2, j, x_first))
 
     def finish(self, j):
         def act(x_first):
-            for d in RING:
-                self.stage2(j, d, x_first).wait_recv()
             value = self.out[pl.ds(3 * j, 3)]
-            for d in range(3):
-                value = value + self.got2[j, d].astype(F32)
+            for way in (0, 1):
+                self.near(2, j, x_first, way).wait_recv()
+                value = value + self.near2[j, way].astype(F32)
             self.out[pl.ds(3 * j, 3)] = value
-            for d in RING:
-                self.stage1(j, d, x_first).wait_send()
-                self.stage2(j, d, x_first).wait_send()
+            for stage in (1, 2):
+                for way in (0, 1):
+                    self.far(stage, j, x_first, way).wait_send()
+                    self.near(stage, j, x_first, way).wait_send()
 
         self.by_axis(j, act)
 
 
-def every_chunk(act):
+def every_chunk(act, start=0, stop=9):
     def step(j, _):
         act(j)
         return 0
 
-    lax.fori_loop(0, 9, step, 0)
+    lax.fori_loop(start, stop, step, 0)
 
 
 def back_columns(stacked, load_w):
@@ -453,8 +534,8 @@
     stacked_in, flipped2, slope, u1_in, u2, w1_in, w2_in,
     grad_in, grad1, grad2,
     u1, f1, f2, adj2, adj1, flipped1,
-    terms2, got2a, mid2, got2b, total2,
-    terms1, got1a, mid1, got1b, total1,
+    terms2, far2a, near2a, mid2, far2b, near2b, total2,
+    terms1, far1a, near1a, mid1, far1b, near1b, total1,
     hid_own, hid_bf, hid_sib, hid_sum, hid_got,
     inp_own, inp_bf, inp_sib, inp_sum, inp_got,
     g2s1, g2r1, g2s2, g2r2, g1s1, g1r1, g1s2, g1r2,
@@ -482,10 +563,10 @@
     )
     halo2.start()
     scatter2 = Scatter(
-        terms2, got2a, mid2, got2b, total2, grad2, x, z, c, (g2s1, g2r1, g2s2, g2r2), 0
+        terms2, far2a, near2a, mid2, far2b, near2b, total2, grad2, x, z, c, (g2s1, g2r1, g2s2, g2r2), 0
     )
     scatter1 = Scatter(
-        terms1, got1a, mid1, got1b, total1, grad1, x, z, c, (g1s1, g1r1, g1s2, g1r2), 1
+        terms1, far1a, near1a, mid1, far1b, near1b, total1, grad1, x, z, c, (g1s1, g1r1, g1s2, g1r2), 1
     )
 
     def second_chunk(j):
@@ -501,7 +582,7 @@
         lax.fori_loop(0, 4, block, 0)
         scatter2.start1(j)
 
-    every_chunk(second_chunk)
+    every_chunk(second_chunk, 0, 4)
     for copy in loads:
         copy.wait()
     halo2.wait_recv()
@@ -516,6 +597,7 @@
         hid_bf[n, 1] = high.astype(BF)
         hid_own[n] = jnp.where(core == 0, low, high)
         hidden_to_sibling(n).start()
+        scatter2.relay1(n)
         return 0
 
     lax.fori_loop(0, 4, hidden_columns, 0)
@@ -533,6 +615,13 @@
             hidden_to_y(d).start()
         else:
             hid_own[n] = pair
+
+    def late_chunk(j):
+        second_chunk(j)
+        pl.when(j < 8)(lambda: scatter2.start2(jnp.maximum(j - 4, 0)))
+        pl.when(j >= 6)(lambda: scatter2.relay1(jnp.maximum(j - 2, 0)))
+
+    every_chunk(late_chunk, 4, 9)
     for d in RING:
         hidden_to_y(d).wait_recv()
     for p in range(4):
@@ -555,7 +644,13 @@
                 terms1[3 * j + k, 2 * n : 2 * n + 2] = turned[:, k * 128 : (k + 1) * 128].reshape(2, 4, 32, 128)
         scatter1.start1(j)
 
-    every_chunk(first_chunk)
+    every_chunk(first_chunk, 0, 3)
+    scatter2.relay1(7)
+    every_chunk(first_chunk, 3, 6)
+    scatter2.relay1(8)
+    every_chunk(first_chunk, 6, 9)
+    every_chunk(scatter1.relay1, 0, 3)
+    every_chunk(scatter2.relay2, 0, 4)
     halo1.wait_recv()
     for n in range(2):
         value = back_columns(adj1, lambda k: f1[k, 2 * n : 2 * n + 2].reshape(256, 128))
@@ -563,6 +658,9 @@
         columns = slice(n * 256, (n + 1) * 256)
         inp_own[:, :, :, :, :, columns] = value
         inp_bf[:, :, :, :, :, columns] = value.astype(BF)
+        if n == 0:
+            every_chunk(scatter1.relay1, 3, 6)
+            every_chunk(scatter2.start2, 4, 6)
     to_sibling = send(inp_bf.at[:, :, 1 - core], inp_sib, iss.at[0], isr.at[0], sibling)
     to_sibling.start()
 
@@ -570,6 +668,7 @@
         n = lax.rem(y + d, 4)
         return send(inp_sum.at[n], inp_got.at[d - 1], iys.at[d - 1], iyr.at[d - 1], (s, n * 2 + core))
 
+    every_chunk(scatter1.relay1, 6, 9)
     to_sibling.wait_recv()
     for d in (1, 3, 2, 0):
         n = lax.rem(y + d, 4)
@@ -579,15 +678,18 @@
             input_to_y(d).start()
         else:
             grad_in[...] = pair
-    every_chunk(scatter2.start2)
+    every_chunk(scatter2.start2, 6, 9)
+    every_chunk(scatter1.start2, 0, 4)
+    every_chunk(scatter2.relay2, 4, 9)
+    every_chunk(scatter1.start2, 4, 9)
     for d in RING:
         input_to_y(d).wait_recv()
     value = grad_in[...]
     for d in range(3):
         value = value + inp_got[d].astype(F32)
     grad_in[...] = value
-    every_chunk(scatter1.start2)
     every_chunk(scatter2.finish)
+    every_chunk(scatter1.relay2)
     every_chunk(scatter1.finish)
 
     halo2.wait_send()
@@ -598,6 +700,11 @@
     for d in RING:
         hidden_to_y(d).wait_send()
         input_to_y(d).wait_send()
+
+
+def hand_over(*refs):
+    for i in range(4):
+        refs[4 + i][...] = refs[i][...]
 
 
 def vmem(count):
@@ -636,7 +743,8 @@
             pltpu.VMEM((27, 4, 4, 32, 128), BF),
             pltpu.VMEM((27, 4, 4, 64, 128), BF),
             pltpu.VMEM((512, 384), F32),
-            dma(2, 16), dma(2, 16), dma(2, 16), dma(2, 16),
+            pltpu.VMEM((1024, 384), F32),
+            dma(2, 5, 4), dma(2, 5, 4), dma(3, 2, 5, 4), dma(3, 2, 5, 4),
             dma(2), dma(2), dma(2), dma(2),
             dma(4), dma(4), dma(4), dma(4), dma(4), dma(4), dma(4), dma(4),
             dma(8),
@@ -664,14 +772,18 @@
             pltpu.VMEM((6, 18, 16, 384), BF),
             pltpu.VMEM((384, 1024), BF),
             pltpu.VMEM((27, 4, 4, 64, 128), BF),
-            pltpu.VMEM((9, 3, 3, 4, 64, 128), BF),
+            pltpu.VMEM((9, 2, 3, 2, 64, 128), BF),
+            pltpu.VMEM((9, 2, 3, 4, 64, 128), BF),
             pltpu.VMEM((9, 3, 4, 64, 128), BF),
-            pltpu.VMEM((9, 3, 3, 64, 128), BF),
+            pltpu.VMEM((9, 2, 3, 32, 128), BF),
+            pltpu.VMEM((9, 2, 3, 64, 128), BF),
             pltpu.VMEM((3, 4, 64, 128), F32),
             pltpu.VMEM((27, 4, 4, 32, 128), BF),
-            pltpu.VMEM((9, 3, 3, 4, 32, 128), BF),
+            pltpu.VMEM((9, 2, 3, 2, 32, 128), BF),
+            pltpu.VMEM((9, 2, 3, 4, 32, 128), BF),
             pltpu.VMEM((9, 3, 4, 32, 128), BF),
-            pltpu.VMEM((9, 3, 3, 32, 128), BF),
+            pltpu.VMEM((9, 2, 3, 16, 128), BF),
+            pltpu.VMEM((9, 2, 3, 32, 128), BF),
             pltpu.VMEM((3, 4, 32, 128), F32),
             pltpu.VMEM((4, 1024, 128), F32),
             pltpu.VMEM((4, 2, 1024, 128), BF),
@@ -683,8 +795,8 @@
             pltpu.VMEM((4, 4, 2, 16, 512), BF),
             pltpu.VMEM((4, 4, 2, 16, 512), BF),
             pltpu.VMEM((3, 4, 2, 16, 512), BF),
-            dma(9, 3), dma(9, 3), dma(9, 3), dma(9, 3),
-            dma(9, 3), dma(9, 3), dma(9, 3), dma(9, 3),
+            dma(9, 4), dma(9, 4), dma(9, 4), dma(9, 4),
+            dma(9, 4), dma(9, 4), dma(9, 4), dma(9, 4),
             dma(2), dma(2), dma(2), dma(2),
             dma(4), dma(4), dma(3), dma(3),
             dma(1), dma(1), dma(3), dma(3),
@@ -695,7 +807,15 @@
         ),
         cost_estimate=pl.CostEstimate(flops=2 * flops, bytes_accessed=40_000_000, transcendentals=0),
     )(stacked, flipped, slope, u1, u2, f1, f2)
-    return (features, grad_input, grad_first, grad_second)
+    results = (features, grad_input, grad_first, grad_second)
+    return pl.pallas_call(
+        hand_over,
+        name="hand_over",
+        out_shape=tuple(shape(r.shape, r.dtype) for r in results),
+        in_specs=vmem(4),
+        out_specs=tuple(vmem(4)),
+        compiler_params=pltpu.CompilerParams(vmem_limit_bytes=VMEM_BYTES),
+    )(*results)
 
 
 def solution(mesh):

time: 204 us -> 171 us (0.84)
  Pallas kernels: 195 us -> 169 us
  local copies, waits for them, and re-layouts: 6.35 us -> 0 us
    pallas_call x1, Pallas kernels: 104 us -> 83.5 us  [local(): pl.pallas_call(forward_kernel, name='forward', out_shape=(shape((4, 16, 1...]
    pallas_call x1, Pallas kernels: 91.7 us -> 83.1 us  [local(): pl.pallas_call(backward_kernel, name='backward', out_shape=(shape((4, 2,...]
    unnamed x6 -> x0, local copies, waits for them, and re-layouts: 6.35 us -> none
    pallas_call x0 -> x1, Pallas kernels: none -> 2.72 us  [local(): pl.pallas_call(hand_over, name='hand_over', out_shape=tuple((shape(r.shap...]
where the time goes in v2:
time: 171 us; the launch traced here: 170 us
  Pallas kernels  169 us (99%)
    pallas_call x1, Pallas kernels, local(): pl.pallas_call(forward_kernel, name='forward', out_shape=(shape((4, 16, 1...  83.5 us
    pallas_call x1, Pallas kernels, local(): pl.pallas_call(backward_kernel, name='backward', out_shape=(shape((4, 2,...  83.1 us

profile of v2, /device:TPU:0, one launch (start us, length us, event | category | flops | bytes accessed | tf_op | source)
XLA Modules:
  0.0 169.9 jit_solution(4732761507205557802)
XLA Ops:
  0.6 83.5 %forward.1 = (bf16[4,16,16,128]{3,2,1,0:T(8,128)(2,1)}, bf16[4,16,16,384]{3,2,1,0:T(8,128)(2,1)}, bf16[384,1024]{1,0:T(8,128)(2,1)}, f32[4,256,128]{2,1,0:T(8,12...) custom-call(bf16[4,2,16,512]{3,2,1,0:T(8,128)(2,1)} %vol.1, ...), custom_call_target="tpu_custom_call" | custom-call | flops 10871635968 | bytes 40000000 | tf_op jit(solution)/shard_map/forward/pallas_call | solution.py:725
  84.1 83.1 %backward.1 = (f32[4,2,16,512]{3,2,1,0:T(8,128)}, f32[27,32,128]{2,1,0:T(8,128)}, f32[27,64,128]{2,1,0:T(8,128)}) custom-call(bf16[4,16,16,384]{3,2,1,0:T(8,128)(2,1)} %get-tuple-element.16.stacked_in, bf16[384,1024]{1,0:T(8,128)(2,1)} %get-tuple-element.17.flipped2, f32[4,256,128]{2,1,0:T(8,128)} %get-tuple-element.18.slope, ...), custom_call_target="tpu_custom_call" | custom-call | flops 21743271936 | bytes 40000000 | tf_op jit(solution)/shard_map/backward/pallas_call | solution.py:757
  167.2 2.7 %hand_over.1 = (bf16[4,16,16,128]{3,2,1,0:T(8,128)(2,1)}, f32[4,2,16,512]{3,2,1,0:T(8,128)}, f32[27,32,128]{2,1,0:T(8,128)}, f32[27,64,128]{2,1,0:T(8,128)}) custom-call(bf16[4,16,16,128]{3,2,1,0:T(8,128)(2,1)} %get-tuple-element.15.refs_0_, f32[4,2,16,512]{3,2,1,0:T(8,128)} %get-tuple-element.23.refs_1_, f32[27,32,128]{2,1,0:T(8,128)} %get-tuple-element.24.refs_2_, ...), custom_call_target="tpu_custom_call" | custom-call | tf_op jit(solution)/shard_map/hand_over/pallas_call | solution.py:811

commit v3 on v2

--- a/solution.py
+++ b/solution.py
@@ -232,38 +232,23 @@
     return sigma * (1.0 + v * (1.0 - sigma))
 
 
-def stack_shifts(v, xp, stacked, x0, y0, flipped):
+def stack_shifts(v, xp, stacked, x0, y0, flipped=None):
     for k, shifted in enumerate((ahead(v), v, behind(v))):
         stacked[xp + x0, y0 : y0 + 16, :, k * 128 : (k + 1) * 128] = shifted.astype(BF).reshape(16, 16, 128)
-        flipped[k * 128 : (k + 1) * 128, xp * 256 : (xp + 1) * 256] = shifted.T.astype(BF)
+        if flipped is not None:
+            flipped[k * 128 : (k + 1) * 128, xp * 256 : (xp + 1) * 256] = shifted.T.astype(BF)
 
 
 def dot(a, b):
     return jnp.dot(a, b, preferred_element_type=F32)
 
 
-def convolve_pair(load, load_w, planes, acc):
-    def step(j, _):
-        a, b = lax.div(j, 3), lax.rem(j, 3)
-        rows = jnp.concatenate([load(p + a, b) for p in planes], axis=0)
-        filters = jnp.concatenate([load_w(3 * j + k) for k in range(3)], axis=1)
-        acc[...] += dot(rows, filters)
-        return 0
-
-    acc[...] = jnp.zeros_like(acc)
-    lax.fori_loop(0, 9, step, 0)
-
-
-def convolve_second(field, filters, acc, a):
-    def step(b, _):
-        rows = jnp.concatenate(
-            [field[q, a : a + 4, pl.ds(b, 16)].reshape(1024, 128) for q in range(8)], axis=1
-        )
-        columns = [filters[9 * a + 3 * b + k].reshape(1024, 128) for k in range(3)]
-        acc[...] += dot(rows, jnp.concatenate(columns, axis=1))
-        return 0
-
-    lax.fori_loop(0, 3, step, 0)
+def convolve_part(load, load_w, a, acc):
+    rows = jnp.concatenate([load(a, b) for b in range(3)], axis=1)
+    filters = jnp.concatenate(
+        [jnp.concatenate([load_w(9 * a + 3 * b + k) for k in range(3)], axis=1) for b in range(3)], axis=0
+    )
+    acc[...] += dot(rows, filters)
 
 
 def plane_of(acc, index):
@@ -274,7 +259,7 @@
 def forward_kernel(
     vol, w1, b1, w2, b2, cot,
     feat, stacked, flipped, slope, u1_out, u2_out, w1_out, w2_out,
-    u1, u2, f1, f2, acc, acc2,
+    u1, u2, f1, f2, acc,
     ag1_s, ag1_r, ag2_s, ag2_r, halo_s, halo_r, hh_s, hh_r, y_s, y_r, c_s, c_r, hy_s, hy_r, hc_s, hc_r, loc,
 ):
     s, c, x, z, y, core = place()
@@ -312,19 +297,20 @@
     first.start_own()
     locals_[0].wait()
     halo.wait_recv()
+    first.near()
     rows.start_own()
-    first.near()
     first.relay(0)
     first.far()
-    rows.forward()
     first.relay(1)
     first.relay(3)
+    rows.forward()
     first.relay(2)
+    rows.finish()
     second[0].start_own()
     second[1].start_own()
-    rows.finish()
     locals_[1].wait()
     locals_[2].wait()
+    acc[...] = jnp.zeros_like(acc)
     first.finish()
     save_u1 = pltpu.make_async_copy(u1, u1_out, loc.at[3])
     save_w1 = pltpu.make_async_copy(f1, w1_out, loc.at[4])
@@ -334,63 +320,84 @@
     hidden_halo = Halo(
         s, c, u2.at[c, 1, 1:17], u2.at[c, 4, 1:17], u2.at[c, 0, 1:17], u2.at[c, 5, 1:17], hh_s, hh_r
     )
-    for planes in ((0, 3), (1, 2)):
-        convolve_pair(
-            lambda p, b: u1[p, pl.ds(b, 16)].reshape(256, 512),
+    for a in range(3):
+        convolve_part(
+            lambda a, b: u1[a : a + 4, b : b + 16].reshape(1024, 512),
             lambda k: f1[k].reshape(512, 128),
-            planes,
+            a,
             acc,
         )
-        for index, p in enumerate(planes):
-            pre = plane_of(acc, index) + b1[...]
-            slope[p] = slope_of(pre)
-            u2[c, p + 1, 1:17] = (pre * jax.nn.sigmoid(pre)).astype(BF).reshape(16, 16, 128)
-        if planes == (0, 3):
+        if a == 0:
+            second[0].near()
+    for p in (0, 3, 1, 2):
+        pre = plane_of(acc, p) + b1[...]
+        slope[p] = slope_of(pre)
+        u2[c, p + 1, 1:17] = (pre * jax.nn.sigmoid(pre)).astype(BF).reshape(16, 16, 128)
+        if p == 3:
             hidden_halo.start()
-            second[0].near()
+            second[2].start_own()
+    channels, low_rim, high_rim = [
+        ChanGather(
+            lambda cb, planes=planes: u2.at[cb, planes, 1:17],
+            s, y, core, hy_s.at[i], hy_r.at[i], hc_s.at[i], hc_r.at[i],
+        )
+        for i, planes in enumerate((slice(1, 5), 0, 5))
+    ]
+    channels.start_own()
+    second[0].relay(3)
+    second[1].near()
+    acc[...] = jnp.zeros_like(acc)
+    second[2].near()
     hidden_halo.wait_recv()
-    channels = ChanGather(lambda cb: u2.at[cb, :, 1:17], s, y, core, hy_s, hy_r, hc_s, hc_r)
-    channels.start_own()
+    low_rim.start_own()
+    high_rim.start_own()
+    second[0].far()
     second[0].relay(0)
-    second[0].far()
-    second[1].near()
-    second[2].start_own()
+    second[1].far()
+    channels.forward()
     second[0].relay(1)
-    second[0].relay(3)
+    second[1].relay(0)
     second[0].relay(2)
-    second[1].relay(0)
-    channels.forward()
-    second[1].far()
-    second[2].near()
+    second[1].relay(3)
+    low_rim.forward()
+    high_rim.forward()
     second[1].relay(1)
-    second[1].relay(3)
+    second[2].far()
     channels.finish()
+    low_rim.finish()
+    high_rim.finish()
     save_u2 = pltpu.make_async_copy(u2, u2_out, loc.at[5])
     save_u2.start()
     second[1].relay(2)
+    second[2].relay(3)
+    second[2].relay(1)
     second[0].finish()
-    acc2[...] = jnp.zeros_like(acc2)
+    second[2].relay(0)
     for a in range(3):
-        convolve_second(u2, f2, acc2, a)
-        if a == 0:
-            second[2].relay(0)
-            second[2].far()
-            second[2].relay(1)
-            second[2].relay(3)
-            second[2].relay(2)
+        convolve_part(
+            lambda a, b: jnp.concatenate(
+                [u2[q, a : a + 4, b : b + 16].reshape(1024, 128) for q in range(8)], axis=1
+            ),
+            lambda k: f2[k].reshape(1024, 128),
+            a,
+            acc,
+        )
         if a < 2:
             second[a + 1].finish()
+        if a == 0:
+            second[2].relay(2)
     save_w2 = pltpu.make_async_copy(f2, w2_out, loc.at[6])
     save_w2.start()
     for p in range(4):
-        pre = plane_of(acc2, p) + b2[...]
+        pre = plane_of(acc, p) + b2[...]
         feat[p] = (pre * jax.nn.sigmoid(pre)).astype(BF).reshape(16, 16, 128)
         adjoint = cot[p].reshape(256, 128).astype(F32) * slope_of(pre)
         stack_shifts(adjoint, p, stacked, 0, 0, flipped)
     halo.wait_send()
     hidden_halo.wait_send()
     rows.wait_send()
-    channels.wait_send()
+    for part in (channels, low_rim, high_rim):
+        part.wait_send()
     first.wait_send()
     for part in second:
         part.wait_send()
@@ -408,6 +415,8 @@
         self.rows = out.shape[1]
 
     def by_axis(self, j, act):
+        if isinstance(j, int):
+            return act((j + self.flip) % 2 == 0)
         x_first = lax.rem(j + self.flip, 2) == 0
 
         @pl.when(x_first)
@@ -533,7 +542,7 @@
 def backward_kernel(
     stacked_in, flipped2, slope, u1_in, u2, w1_in, w2_in,
     grad_in, grad1, grad2,
-    u1, f1, f2, adj2, adj1, flipped1,
+    u1, f1, f2, adj2, adj1, flipped1, rim2, rim1,
     terms2, far2a, near2a, mid2, far2b, near2b, total2,
     terms1, far1a, near1a, mid1, far1b, near1b, total1,
     hid_own, hid_bf, hid_sib, hid_sum, hid_got,
@@ -551,16 +560,23 @@
     for copy in loads:
         copy.start()
     for field in (adj2, adj1):
-        for plane in (0, 5):
-            field[plane] = jnp.zeros((18, 16, 384), BF)
         for row in (0, 17):
-            field[1:5, row] = jnp.zeros((4, 16, 384), BF)
+            field[:, row] = jnp.zeros((6, 16, 384), BF)
+    for rim in (rim2, rim1):
+        rim[...] = jnp.zeros_like(rim)
     greet(s, c, x, z)
     sibling = (s, y * 2 + 1 - core)
 
+    middle = slice(128, 256)
     halo2 = Halo(
-        s, c, stacked_in.at[0], stacked_in.at[3], adj2.at[0, 1:17], adj2.at[5, 1:17], h2s, h2r
+        s, c, stacked_in.at[0, :, :, middle], stacked_in.at[3, :, :, middle], rim2.at[0], rim2.at[1], h2s, h2r
     )
+
+    def take_rims(halo, rim, field):
+        halo.wait_recv()
+        for side, plane in ((0, 0), (1, 5)):
+            stack_shifts(rim[side].reshape(256, 128).astype(F32), plane, field, 0, 1)
+
     halo2.start()
     scatter2 = Scatter(
         terms2, far2a, near2a, mid2, far2b, near2b, total2, grad2, x, z, c, (g2s1, g2r1, g2s2, g2r2), 0
@@ -572,56 +588,61 @@
     def second_chunk(j):
         a, b = lax.div(j, 3), lax.rem(j, 3)
 
-        def block(n, _):
-            fields = [u2[2 * n + q, pl.ds(a, 4), pl.ds(b, 16)].reshape(1024, 128) for q in range(2)]
-            turned = dot(flipped2[...], jnp.concatenate(fields, axis=1)).T.astype(BF)
-            for k in range(3):
-                terms2[3 * j + k, n] = turned[:, k * 128 : (k + 1) * 128].reshape(4, 64, 128)
-            return 0
-
-        lax.fori_loop(0, 4, block, 0)
+        fields = [u2[q, pl.ds(a, 4), pl.ds(b, 16)].reshape(1024, 128) for q in range(8)]
+        turned = dot(flipped2[...], jnp.concatenate(fields, axis=1)).T.astype(BF)
+        for k in range(3):
+            terms2[3 * j + k] = turned[:, k * 128 : (k + 1) * 128].reshape(4, 4, 64, 128)
         scatter2.start1(j)
 
-    every_chunk(second_chunk, 0, 4)
+    every_chunk(second_chunk, 0, 6)
     for copy in loads:
         copy.wait()
-    halo2.wait_recv()
+    take_rims(halo2, rim2, adj2)
+    scatter2.relay1(0)
+    scatter2.relay1(1)
 
     def hidden_to_sibling(n):
         return send(hid_bf.at[n, 1 - core], hid_sib.at[n], hss.at[n], hsr.at[n], sibling)
 
-    def hidden_columns(n, _):
+    def hidden_to_y(d):
+        n = lax.rem(y + d, 4)
+        return send(hid_sum.at[n], hid_got.at[d - 1], hys.at[d - 1], hyr.at[d - 1], (s, n * 2 + core))
+
+    def hidden_pair(n):
+        hidden_to_sibling(n).wait_recv()
+        return hid_own[n] + hid_sib[n].astype(F32)
+
+    def hidden_columns(i, _):
+        n = lax.rem(y + 1 + i, 4)
+        pl.when(i < 3)(lambda: second_chunk(jnp.minimum(6 + i, 8)))
         value = back_columns(adj2, lambda k: f2[k, n].reshape(256, 128))
         low, high = value[:, :128], value[:, 128:]
         hid_bf[n, 0] = low.astype(BF)
         hid_bf[n, 1] = high.astype(BF)
         hid_own[n] = jnp.where(core == 0, low, high)
         hidden_to_sibling(n).start()
-        scatter2.relay1(n)
+
+        @pl.when(i > 0)
+        def _():
+            d = jnp.maximum(i, 1)
+            before = lax.rem(y + d, 4)
+            hid_sum[before] = hidden_pair(before).astype(BF)
+            hidden_to_y(d).start()
+
+        @pl.when(i < 3)
+        def _():
+            scatter2.relay1(2 * jnp.minimum(i, 2) + 2)
+            scatter2.relay1(2 * jnp.minimum(i, 2) + 3)
+
+        pl.when(i > 0)(lambda: scatter2.start2(jnp.maximum(i - 1, 0)))
         return 0
 
     lax.fori_loop(0, 4, hidden_columns, 0)
-
-    def hidden_to_y(d):
-        n = lax.rem(y + d, 4)
-        return send(hid_sum.at[n], hid_got.at[d - 1], hys.at[d - 1], hyr.at[d - 1], (s, n * 2 + core))
-
-    for d in (1, 3, 2, 0):
-        n = lax.rem(y + d, 4)
-        hidden_to_sibling(n).wait_recv()
-        pair = hid_own[n] + hid_sib[n].astype(F32)
-        if d:
-            hid_sum[n] = pair.astype(BF)
-            hidden_to_y(d).start()
-        else:
-            hid_own[n] = pair
-
-    def late_chunk(j):
-        second_chunk(j)
-        pl.when(j < 8)(lambda: scatter2.start2(jnp.maximum(j - 4, 0)))
-        pl.when(j >= 6)(lambda: scatter2.relay1(jnp.maximum(j - 2, 0)))
-
-    every_chunk(late_chunk, 4, 9)
+    hid_own[y] = hidden_pair(y)
+
+    scatter2.start2(3)
+    scatter2.start2(4)
+    scatter2.relay1(8)
     for d in RING:
         hidden_to_y(d).wait_recv()
     for p in range(4):
@@ -631,27 +652,28 @@
             value = value + hid_got[d, rows].astype(F32)
         stack_shifts(value * slope[p], p, adj1, 1, 1, flipped1)
     halo1 = Halo(
-        s, c, adj1.at[1, 1:17], adj1.at[4, 1:17], adj1.at[0, 1:17], adj1.at[5, 1:17], h1s, h1r
+        s, c, adj1.at[1, 1:17, :, middle], adj1.at[4, 1:17, :, middle], rim1.at[0], rim1.at[1], h1s, h1r
     )
     halo1.start()
+    scatter2.relay2(0)
+    scatter2.relay2(1)
 
     def first_chunk(j):
         a, b = lax.div(j, 3), lax.rem(j, 3)
-        for n in range(2):
-            field = u1[pl.ds(a, 4), pl.ds(b, 16), :, n * 256 : (n + 1) * 256].reshape(1024, 256)
-            turned = dot(flipped1[...], field).T.astype(BF)
-            for k in range(3):
-                terms1[3 * j + k, 2 * n : 2 * n + 2] = turned[:, k * 128 : (k + 1) * 128].reshape(2, 4, 32, 128)
+        field = u1[pl.ds(a, 4), pl.ds(b, 16)].reshape(1024, 512)
+        turned = dot(flipped1[...], field).T.astype(BF)
+        for k in range(3):
+            terms1[3 * j + k] = turned[:, k * 128 : (k + 1) * 128].reshape(4, 4, 32, 128)
         scatter1.start1(j)
 
-    every_chunk(first_chunk, 0, 3)
-    scatter2.relay1(7)
-    every_chunk(first_chunk, 3, 6)
-    scatter2.relay1(8)
-    every_chunk(first_chunk, 6, 9)
-    every_chunk(scatter1.relay1, 0, 3)
-    every_chunk(scatter2.relay2, 0, 4)
-    halo1.wait_recv()
+    def first_step(j):
+        first_chunk(j)
+        pl.when(j > 4)(lambda: scatter1.relay1(jnp.maximum(j - 5, 0)))
+
+    every_chunk(first_step)
+    scatter2.start2(5)
+    take_rims(halo1, rim1, adj1)
+    scatter1.relay1(4)
     for n in range(2):
         value = back_columns(adj1, lambda k: f1[k, 2 * n : 2 * n + 2].reshape(256, 128))
         value = value.reshape(4, 4, 2, 2, 16, 256)
@@ -659,8 +681,10 @@
         inp_own[:, :, :, :, :, columns] = value
         inp_bf[:, :, :, :, :, columns] = value.astype(BF)
         if n == 0:
-            every_chunk(scatter1.relay1, 3, 6)
-            every_chunk(scatter2.start2, 4, 6)
+            scatter1.start2(0)
+            for j in (5, 6, 7):
+                scatter1.relay1(j)
+            scatter2.start2(6)
     to_sibling = send(inp_bf.at[:, :, 1 - core], inp_sib, iss.at[0], isr.at[0], sibling)
     to_sibling.start()
 
@@ -668,7 +692,12 @@
         n = lax.rem(y + d, 4)
         return send(inp_sum.at[n], inp_got.at[d - 1], iys.at[d - 1], iyr.at[d - 1], (s, n * 2 + core))
 
-    every_chunk(scatter1.relay1, 6, 9)
+    scatter1.relay1(8)
+    scatter2.relay2(2)
+    scatter2.relay2(3)
+    scatter1.start2(1)
+    scatter1.start2(2)
+    scatter2.start2(7)
     to_sibling.wait_recv()
     for d in (1, 3, 2, 0):
         n = lax.rem(y + d, 4)
@@ -678,19 +707,36 @@
             input_to_y(d).start()
         else:
             grad_in[...] = pair
-    every_chunk(scatter2.start2, 6, 9)
-    every_chunk(scatter1.start2, 0, 4)
-    every_chunk(scatter2.relay2, 4, 9)
-    every_chunk(scatter1.start2, 4, 9)
+    for j in (3, 4, 5):
+        scatter1.start2(j)
+    scatter1.relay2(0)
+    scatter2.relay2(4)
+    scatter1.relay2(1)
+    scatter2.start2(8)
+    scatter1.start2(6)
+    scatter1.relay2(2)
+    scatter2.relay2(5)
+    scatter1.start2(7)
+    scatter1.relay2(3)
+    scatter2.relay2(6)
+    scatter1.start2(8)
+    scatter1.relay2(4)
+    scatter1.relay2(5)
+    scatter2.relay2(7)
+    scatter1.relay2(6)
+    scatter2.relay2(8)
+    scatter1.relay2(7)
+    scatter1.relay2(8)
+    every_chunk(scatter2.finish, 0, 7)
     for d in RING:
         input_to_y(d).wait_recv()
     value = grad_in[...]
     for d in range(3):
         value = value + inp_got[d].astype(F32)
     grad_in[...] = value
-    every_chunk(scatter2.finish)
-    every_chunk(scatter1.relay2)
-    every_chunk(scatter1.finish)
+    every_chunk(scatter1.finish, 0, 6)
+    every_chunk(scatter2.finish, 7, 9)
+    every_chunk(scatter1.finish, 6, 9)
 
     halo2.wait_send()
     halo1.wait_send()
@@ -742,11 +788,10 @@
             pltpu.VMEM((8, 6, 18, 16, 128), BF),
             pltpu.VMEM((27, 4, 4, 32, 128), BF),
             pltpu.VMEM((27, 4, 4, 64, 128), BF),
-            pltpu.VMEM((512, 384), F32),
             pltpu.VMEM((1024, 384), F32),
             dma(2, 5, 4), dma(2, 5, 4), dma(3, 2, 5, 4), dma(3, 2, 5, 4),
             dma(2), dma(2), dma(2), dma(2),
-            dma(4), dma(4), dma(4), dma(4), dma(4), dma(4), dma(4), dma(4),
+            dma(4), dma(4), dma(4), dma(4), dma(3, 4), dma(3, 4), dma(3, 4), dma(3, 4),
             dma(8),
         ],
         compiler_params=pltpu.CompilerParams(
@@ -771,6 +816,8 @@
             pltpu.VMEM((6, 18, 16, 384), BF),
             pltpu.VMEM((6, 18, 16, 384), BF),
             pltpu.VMEM((384, 1024), BF),
+            pltpu.VMEM((2, 16, 16, 128), BF),
+            pltpu.VMEM((2, 16, 16, 128), BF),
             pltpu.VMEM((27, 4, 4, 64, 128), BF),
             pltpu.VMEM((9, 2, 3, 2, 64, 128), BF),
             pltpu.VMEM((9, 2, 3, 4, 64, 128), BF),

time: 171 us -> 155 us (0.906)
  Pallas kernels: 169 us -> 154 us
    pallas_call x1, Pallas kernels: 83.1 us -> 73.1 us  [local(): pl.pallas_call(backward_kernel, name='backward', out_shape=(shape((4, 2,...]
    pallas_call x1, Pallas kernels: 83.5 us -> 78.4 us  [local(): pl.pallas_call(forward_kernel, name='forward', out_shape=(shape((4, 16, 1...]
where the time goes in v3:
time: 155 us
  Pallas kernels  154 us (99%)
    pallas_call x1, Pallas kernels, local(): pl.pallas_call(forward_kernel, name='forward', out_shape=(shape((4, 16, 1...  78.4 us
    pallas_call x1, Pallas kernels, local(): pl.pallas_call(backward_kernel, name='backward', out_shape=(shape((4, 2,...  73.1 us

profile of v3, /device:TPU:0, one launch (start us, length us, event | category | flops | bytes accessed | tf_op | source)
XLA Modules:
  0.0 154.8 jit_solution(3423445460717337185)
XLA Ops:
  0.6 78.4 %forward.1 = (bf16[4,16,16,128]{3,2,1,0:T(8,128)(2,1)}, bf16[4,16,16,384]{3,2,1,0:T(8,128)(2,1)}, bf16[384,1024]{1,0:T(8,128)(2,1)}, f32[4,256,128]{2,1,0:T(8,12...) custom-call(bf16[4,2,16,512]{3,2,1,0:T(8,128)(2,1)} %vol.1, ...), custom_call_target="tpu_custom_call" | custom-call | flops 10871635968 | bytes 40000000 | tf_op jit(solution)/shard_map/forward/pallas_call | solution.py:771
  79.0 73.1 %backward.1 = (f32[4,2,16,512]{3,2,1,0:T(8,128)}, f32[27,32,128]{2,1,0:T(8,128)}, f32[27,64,128]{2,1,0:T(8,128)}) custom-call(bf16[4,16,16,384]{3,2,1,0:T(8,128)(2,1)} %get-tuple-element.16.stacked_in, bf16[384,1024]{1,0:T(8,128)(2,1)} %get-tuple-element.17.flipped2, f32[4,256,128]{2,1,0:T(8,128)} %get-tuple-element.18.slope, ...), custom_call_target="tpu_custom_call" | custom-call | flops 21743271936 | bytes 40000000 | tf_op jit(solution)/shard_map/backward/pallas_call | solution.py:802
  152.1 2.7 %hand_over.1 = (bf16[4,16,16,128]{3,2,1,0:T(8,128)(2,1)}, f32[4,2,16,512]{3,2,1,0:T(8,128)}, f32[27,32,128]{2,1,0:T(8,128)}, f32[27,64,128]{2,1,0:T(8,128)}) custom-call(bf16[4,16,16,128]{3,2,1,0:T(8,128)(2,1)} %get-tuple-element.15.refs_0_, f32[4,2,16,512]{3,2,1,0:T(8,128)} %get-tuple-element.23.refs_1_, f32[27,32,128]{2,1,0:T(8,128)} %get-tuple-element.24.refs_2_, ...), custom_call_target="tpu_custom_call" | custom-call | tf_op jit(solution)/shard_map/hand_over/pallas_call | solution.py:858

commit v4 on v3

--- a/solution.py
+++ b/solution.py
@@ -256,11 +256,152 @@
     return behind(acc[rows, 0:128]) + acc[rows, 128:256] + ahead(acc[rows, 256:384])
 
 
-def forward_kernel(
+class Scatter:
+    def __init__(self, terms, far1, near1, mid, far2, near2, total, out, x, z, c, sems, flip):
+        self.terms, self.far1, self.near1 = terms, far1, near1
+        self.mid, self.far2, self.near2 = mid, far2, near2
+        self.total, self.out = total, out
+        self.x, self.z, self.c, self.flip = x, z, c, flip
+        self.s1, self.r1, self.s2, self.r2 = sems
+        self.rows = out.shape[1]
+
+    def by_axis(self, j, act):
+        if isinstance(j, int):
+            return act((j + self.flip) % 2 == 0)
+        x_first = lax.rem(j + self.flip, 2) == 0
+
+        @pl.when(x_first)
+        def _():
+            act(True)
+
+        @pl.when(jnp.logical_not(x_first))
+        def _():
+            act(False)
+
+    def target(self, along_x, d):
+        tx = lax.rem(self.x + d, 4) if along_x else self.x
+        tz = self.z if along_x else lax.rem(self.z + d, 4)
+        return tx * 4 + tz, self.c
+
+    def block1(self, j, x_first, d, part=None):
+        offsets = pl.ds(3 * j, 3)
+        if x_first:
+            lead = (offsets, lax.rem(self.x + d, 4))
+            return lead if part is None else lead + (slice(2 * part, 2 * part + 2),)
+        at = lax.rem(self.z + d, 4)
+        return (offsets, slice(None) if part is None else slice(2 * part, 2 * part + 2), at)
+
+    def block2(self, j, x_first, d, part=None):
+        at = lax.rem((self.z if x_first else self.x) + d, 4)
+        half = self.rows // 2
+        lead = (j, slice(None), at)
+        return lead if part is None else lead + (slice(half * part, half * (part + 1)),)
+
+    def far(self, stage, j, x_first, way):
+        src, dst = (
+            (self.terms.at[self.block1(j, x_first, 2, way)], self.far1)
+            if stage == 1
+            else (self.mid.at[self.block2(j, x_first, 2, way)], self.far2)
+        )
+        s, r = (self.s1, self.r1) if stage == 1 else (self.s2, self.r2)
+        to = self.target(x_first == (stage == 1), (1, 3)[way])
+        return send(src, dst.at[j, way], s.at[j, way], r.at[j, way], to)
+
+    def near(self, stage, j, x_first, way):
+        step = (1, 3)[way]
+        src, dst = (
+            (self.terms.at[self.block1(j, x_first, step)], self.near1)
+            if stage == 1
+            else (self.mid.at[self.block2(j, x_first, step)], self.near2)
+        )
+        s, r = (self.s1, self.r1) if stage == 1 else (self.s2, self.r2)
+        to = self.target(x_first == (stage == 1), step)
+        return send(src, dst.at[j, way], s.at[j, 2 + way], r.at[j, 2 + way], to)
+
+    def pass_on(self, stage, j, x_first):
+        for way, step in ((0, 1), (1, 3)):
+            self.far(stage, j, x_first, way).wait_recv()
+            if stage == 1:
+                field, got, where = self.terms, self.far1, self.block1(j, x_first, step, way)
+            else:
+                field, got, where = self.mid, self.far2, self.block2(j, x_first, step, way)
+            field[where] = (field[where].astype(F32) + got[j, way].astype(F32)).astype(BF)
+            self.near(stage, j, x_first, way).start()
+
+    def start1(self, j):
+        def act(x_first):
+            self.far(1, j, x_first, 0).start()
+            self.far(1, j, x_first, 1).start()
+
+        self.by_axis(j, act)
+
+    def relay1(self, j):
+        self.by_axis(j, lambda x_first: self.pass_on(1, j, x_first))
+
+    def start2(self, j):
+        def act(x_first):
+            value = self.terms[self.block1(j, x_first, 0)].astype(F32)
+            for way in (0, 1):
+                self.near(1, j, x_first, way).wait_recv()
+                value = value + self.near1[j, way].astype(F32)
+            self.total[...] = value
+            self.mid[j] = value.astype(BF)
+            self.far(2, j, x_first, 0).start()
+            self.far(2, j, x_first, 1).start()
+            self.out[pl.ds(3 * j, 3)] = self.total[:, self.z] if x_first else self.total[:, self.x]
+
+        self.by_axis(j, act)
+
+    def relay2(self, j):
+        self.by_axis(j, lambda x_first: self.pass_on(2, j, x_first))
+
+    def finish(self, j):
+        def act(x_first):
+            value = self.out[pl.ds(3 * j, 3)]
+            for way in (0, 1):
+                self.near(2, j, x_first, way).wait_recv()
+                value = value + self.near2[j, way].astype(F32)
+            self.out[pl.ds(3 * j, 3)] = value
+            for stage in (1, 2):
+                for way in (0, 1):
+                    self.far(stage, j, x_first, way).wait_send()
+                    self.near(stage, j, x_first, way).wait_send()
+
+        self.by_axis(j, act)
+
+
+def every_chunk(act, start=0, stop=9):
+    def step(j, _):
+        act(j)
+        return 0
+
+    lax.fori_loop(start, stop, step, 0)
+
+
+def back_columns(stacked, load_w):
+    total = None
+    for a in range(3):
+        rows = jnp.concatenate(
+            [stacked[2 - a : 6 - a, 2 - b : 18 - b].reshape(1024, 384) for b in range(3)], axis=1
+        )
+        filters = jnp.concatenate([load_w(9 * a + k) for k in range(9)], axis=1)
+        term = lax.dot_general(rows, filters, (((1,), (1,)), ((), ())), preferred_element_type=F32)
+        total = term if total is None else total + term
+    return total
+
+
+def step_kernel(
     vol, w1, b1, w2, b2, cot,
-    feat, stacked, flipped, slope, u1_out, u2_out, w1_out, w2_out,
-    u1, u2, f1, f2, acc,
+    feat, grad_in, grad1, grad2,
+    u1, u2, f1, f2, acc, slope,
+    adj2, adj1, flipped2, flipped1, rim2, rim1,
+    terms2, far2a, near2a, mid2, far2b, near2b, total2,
+    terms1, far1a, near1a, mid1, far1b, near1b, total1,
+    hid_own, hid_bf, hid_sib, hid_sum, hid_got,
+    inp_own, inp_bf, inp_sib, inp_sum, inp_got,
     ag1_s, ag1_r, ag2_s, ag2_r, halo_s, halo_r, hh_s, hh_r, y_s, y_r, c_s, c_r, hy_s, hy_r, hc_s, hc_r, loc,
+    g2s1, g2r1, g2s2, g2r2, g1s1, g1r1, g1s2, g1r2,
+    h2s, h2r, h1s, h1r, hss, hsr, hys, hyr, iss, isr, iys, iyr,
 ):
     s, c, x, z, y, core = place()
     u1[0] = jnp.zeros((18, 16, 512), BF)
@@ -276,6 +417,11 @@
         return 0
 
     lax.fori_loop(0, 8, clear, 0)
+    for field in (adj2, adj1):
+        for row in (0, 17):
+            field[:, row] = jnp.zeros((6, 16, 384), BF)
+    for rim in (rim2, rim1):
+        rim[...] = jnp.zeros_like(rim)
     rows_of = lambda cb: u1.at[:, pl.ds(1 + 2 * cb, 2)]
     locals_ = [
         pltpu.make_async_copy(vol, u1.at[1:5, pl.ds(1 + 2 * c, 2)], loc.at[0]),
@@ -292,30 +438,26 @@
         s, c, vol.at[0], vol.at[3],
         u1.at[0, pl.ds(1 + 2 * c, 2)], u1.at[5, pl.ds(1 + 2 * c, 2)], halo_s, halo_r,
     )
-    rows = ChanGather(rows_of, s, y, core, y_s, y_r, c_s, c_r)
+    voxels = ChanGather(rows_of, s, y, core, y_s, y_r, c_s, c_r)
     halo.start()
     first.start_own()
     locals_[0].wait()
     halo.wait_recv()
     first.near()
-    rows.start_own()
+    voxels.start_own()
     first.relay(0)
     first.far()
     first.relay(1)
     first.relay(3)
-    rows.forward()
+    voxels.forward()
     first.relay(2)
-    rows.finish()
+    voxels.finish()
     second[0].start_own()
     second[1].start_own()
     locals_[1].wait()
     locals_[2].wait()
     acc[...] = jnp.zeros_like(acc)
     first.finish()
-    save_u1 = pltpu.make_async_copy(u1, u1_out, loc.at[3])
-    save_w1 = pltpu.make_async_copy(f1, w1_out, loc.at[4])
-    save_u1.start()
-    save_w1.start()
 
     hidden_halo = Halo(
         s, c, u2.at[c, 1, 1:17], u2.at[c, 4, 1:17], u2.at[c, 0, 1:17], u2.at[c, 5, 1:17], hh_s, hh_r
@@ -366,8 +508,6 @@
     channels.finish()
     low_rim.finish()
     high_rim.finish()
-    save_u2 = pltpu.make_async_copy(u2, u2_out, loc.at[5])
-    save_u2.start()
     second[1].relay(2)
     second[2].relay(3)
     second[2].relay(1)
@@ -386,198 +526,24 @@
             second[a + 1].finish()
         if a == 0:
             second[2].relay(2)
-    save_w2 = pltpu.make_async_copy(f2, w2_out, loc.at[6])
-    save_w2.start()
-    for p in range(4):
+    middle = slice(128, 256)
+    halo2 = Halo(
+        s, c, adj2.at[1, 1:17, :, middle], adj2.at[4, 1:17, :, middle], rim2.at[0], rim2.at[1], h2s, h2r
+    )
+    for p in (0, 3, 1, 2):
         pre = plane_of(acc, p) + b2[...]
         feat[p] = (pre * jax.nn.sigmoid(pre)).astype(BF).reshape(16, 16, 128)
         adjoint = cot[p].reshape(256, 128).astype(F32) * slope_of(pre)
-        stack_shifts(adjoint, p, stacked, 0, 0, flipped)
-    halo.wait_send()
-    hidden_halo.wait_send()
-    rows.wait_send()
-    for part in (channels, low_rim, high_rim):
-        part.wait_send()
-    first.wait_send()
-    for part in second:
-        part.wait_send()
-    for copy in (save_u1, save_w1, save_u2, save_w2):
-        copy.wait()
-
-
-class Scatter:
-    def __init__(self, terms, far1, near1, mid, far2, near2, total, out, x, z, c, sems, flip):
-        self.terms, self.far1, self.near1 = terms, far1, near1
-        self.mid, self.far2, self.near2 = mid, far2, near2
-        self.total, self.out = total, out
-        self.x, self.z, self.c, self.flip = x, z, c, flip
-        self.s1, self.r1, self.s2, self.r2 = sems
-        self.rows = out.shape[1]
-
-    def by_axis(self, j, act):
-        if isinstance(j, int):
-            return act((j + self.flip) % 2 == 0)
-        x_first = lax.rem(j + self.flip, 2) == 0
-
-        @pl.when(x_first)
-        def _():
-            act(True)
-
-        @pl.when(jnp.logical_not(x_first))
-        def _():
-            act(False)
-
-    def target(self, along_x, d):
-        tx = lax.rem(self.x + d, 4) if along_x else self.x
-        tz = self.z if along_x else lax.rem(self.z + d, 4)
-        return tx * 4 + tz, self.c
-
-    def block1(self, j, x_first, d, part=None):
-        offsets = pl.ds(3 * j, 3)
-        if x_first:
-            lead = (offsets, lax.rem(self.x + d, 4))
-            return lead if part is None else lead + (slice(2 * part, 2 * part + 2),)
-        at = lax.rem(self.z + d, 4)
-        return (offsets, slice(None) if part is None else slice(2 * part, 2 * part + 2), at)
-
-    def block2(self, j, x_first, d, part=None):
-        at = lax.rem((self.z if x_first else self.x) + d, 4)
-        half = self.rows // 2
-        lead = (j, slice(None), at)
-        return lead if part is None else lead + (slice(half * part, half * (part + 1)),)
-
-    def far(self, stage, j, x_first, way):
-        src, dst = (
-            (self.terms.at[self.block1(j, x_first, 2, way)], self.far1)
-            if stage == 1
-            else (self.mid.at[self.block2(j, x_first, 2, way)], self.far2)
-        )
-        s, r = (self.s1, self.r1) if stage == 1 else (self.s2, self.r2)
-        to = self.target(x_first == (stage == 1), (1, 3)[way])
-        return send(src, dst.at[j, way], s.at[j, way], r.at[j, way], to)
-
-    def near(self, stage, j, x_first, way):
-        step = (1, 3)[way]
-        src, dst = (
-            (self.terms.at[self.block1(j, x_first, step)], self.near1)
-            if stage == 1
-            else (self.mid.at[self.block2(j, x_first, step)], self.near2)
-        )
-        s, r = (self.s1, self.r1) if stage == 1 else (self.s2, self.r2)
-        to = self.target(x_first == (stage == 1), step)
-        return send(src, dst.at[j, way], s.at[j, 2 + way], r.at[j, 2 + way], to)
-
-    def pass_on(self, stage, j, x_first):
-        for way, step in ((0, 1), (1, 3)):
-            self.far(stage, j, x_first, way).wait_recv()
-            if stage == 1:
-                field, got, where = self.terms, self.far1, self.block1(j, x_first, step, way)
-            else:
-                field, got, where = self.mid, self.far2, self.block2(j, x_first, step, way)
-            field[where] = (field[where].astype(F32) + got[j, way].astype(F32)).astype(BF)
-            self.near(stage, j, x_first, way).start()
-
-    def start1(self, j):
-        def act(x_first):
-            self.far(1, j, x_first, 0).start()
-            self.far(1, j, x_first, 1).start()
-
-        self.by_axis(j, act)
-
-    def relay1(self, j):
-        self.by_axis(j, lambda x_first: self.pass_on(1, j, x_first))
-
-    def start2(self, j):
-        def act(x_first):
-            value = self.terms[self.block1(j, x_first, 0)].astype(F32)
-            for way in (0, 1):
-                self.near(1, j, x_first, way).wait_recv()
-                value = value + self.near1[j, way].astype(F32)
-            self.total[...] = value
-            self.mid[j] = value.astype(BF)
-            self.far(2, j, x_first, 0).start()
-            self.far(2, j, x_first, 1).start()
-            self.out[pl.ds(3 * j, 3)] = self.total[:, self.z] if x_first else self.total[:, self.x]
-
-        self.by_axis(j, act)
-
-    def relay2(self, j):
-        self.by_axis(j, lambda x_first: self.pass_on(2, j, x_first))
-
-    def finish(self, j):
-        def act(x_first):
-            value = self.out[pl.ds(3 * j, 3)]
-            for way in (0, 1):
-                self.near(2, j, x_first, way).wait_recv()
-                value = value + self.near2[j, way].astype(F32)
-            self.out[pl.ds(3 * j, 3)] = value
-            for stage in (1, 2):
-                for way in (0, 1):
-                    self.far(stage, j, x_first, way).wait_send()
-                    self.near(stage, j, x_first, way).wait_send()
-
-        self.by_axis(j, act)
-
-
-def every_chunk(act, start=0, stop=9):
-    def step(j, _):
-        act(j)
-        return 0
-
-    lax.fori_loop(start, stop, step, 0)
-
-
-def back_columns(stacked, load_w):
-    total = None
-    for a in range(3):
-        rows = jnp.concatenate(
-            [stacked[2 - a : 6 - a, 2 - b : 18 - b].reshape(1024, 384) for b in range(3)], axis=1
-        )
-        filters = jnp.concatenate([load_w(9 * a + k) for k in range(9)], axis=1)
-        term = lax.dot_general(rows, filters, (((1,), (1,)), ((), ())), preferred_element_type=F32)
-        total = term if total is None else total + term
-    return total
-
-
-def backward_kernel(
-    stacked_in, flipped2, slope, u1_in, u2, w1_in, w2_in,
-    grad_in, grad1, grad2,
-    u1, f1, f2, adj2, adj1, flipped1, rim2, rim1,
-    terms2, far2a, near2a, mid2, far2b, near2b, total2,
-    terms1, far1a, near1a, mid1, far1b, near1b, total1,
-    hid_own, hid_bf, hid_sib, hid_sum, hid_got,
-    inp_own, inp_bf, inp_sib, inp_sum, inp_got,
-    g2s1, g2r1, g2s2, g2r2, g1s1, g1r1, g1s2, g1r2,
-    h2s, h2r, h1s, h1r, hss, hsr, hys, hyr, iss, isr, iys, iyr, loc,
-):
-    s, c, x, z, y, core = place()
-    loads = [
-        pltpu.make_async_copy(stacked_in, adj2.at[1:5, 1:17], loc.at[0]),
-        pltpu.make_async_copy(w2_in, f2, loc.at[1]),
-        pltpu.make_async_copy(u1_in, u1, loc.at[2]),
-        pltpu.make_async_copy(w1_in, f1, loc.at[3]),
-    ]
-    for copy in loads:
-        copy.start()
-    for field in (adj2, adj1):
-        for row in (0, 17):
-            field[:, row] = jnp.zeros((6, 16, 384), BF)
-    for rim in (rim2, rim1):
-        rim[...] = jnp.zeros_like(rim)
-    greet(s, c, x, z)
+        stack_shifts(adjoint, p, adj2, 1, 1, flipped2)
+        if p == 3:
+            halo2.start()
     sibling = (s, y * 2 + 1 - core)
-
-    middle = slice(128, 256)
-    halo2 = Halo(
-        s, c, stacked_in.at[0, :, :, middle], stacked_in.at[3, :, :, middle], rim2.at[0], rim2.at[1], h2s, h2r
-    )
 
     def take_rims(halo, rim, field):
         halo.wait_recv()
         for side, plane in ((0, 0), (1, 5)):
             stack_shifts(rim[side].reshape(256, 128).astype(F32), plane, field, 0, 1)
 
-    halo2.start()
     scatter2 = Scatter(
         terms2, far2a, near2a, mid2, far2b, near2b, total2, grad2, x, z, c, (g2s1, g2r1, g2s2, g2r2), 0
     )
@@ -595,8 +561,6 @@
         scatter2.start1(j)
 
     every_chunk(second_chunk, 0, 6)
-    for copy in loads:
-        copy.wait()
     take_rims(halo2, rim2, adj2)
     scatter2.relay1(0)
     scatter2.relay1(1)
@@ -746,6 +710,14 @@
     for d in RING:
         hidden_to_y(d).wait_send()
         input_to_y(d).wait_send()
+    halo.wait_send()
+    hidden_halo.wait_send()
+    voxels.wait_send()
+    for part in (channels, low_rim, high_rim):
+        part.wait_send()
+    first.wait_send()
+    for part in second:
+        part.wait_send()
 
 
 def hand_over(*refs):
@@ -768,70 +740,41 @@
 def local(volume, w_first, b_first, w_second, b_second, cotangent):
     shape = jax.ShapeDtypeStruct
     flops = 2 * 1024 * 27 * 128 * 1536
-    features, stacked, flipped, slope, u1, u2, f1, f2 = pl.pallas_call(
-        forward_kernel,
-        name="forward",
+    half_banks = lambda rows: [
+        pltpu.VMEM((27, 4, 4, rows, 128), BF),
+        pltpu.VMEM((9, 2, 3, 2, rows, 128), BF),
+        pltpu.VMEM((9, 2, 3, 4, rows, 128), BF),
+        pltpu.VMEM((9, 3, 4, rows, 128), BF),
+        pltpu.VMEM((9, 2, 3, rows // 2, 128), BF),
+        pltpu.VMEM((9, 2, 3, rows, 128), BF),
+        pltpu.VMEM((3, 4, rows, 128), F32),
+    ]
+    features, grad_input, grad_first, grad_second = pl.pallas_call(
+        step_kernel,
+        name="forward_backward",
         out_shape=(
             shape((4, 16, 16, 128), BF),
-            shape((4, 16, 16, 384), BF),
-            shape((384, 1024), BF),
-            shape((4, 256, 128), F32),
-            shape((6, 18, 16, 512), BF),
-            shape((8, 6, 18, 16, 128), BF),
-            shape((27, 4, 4, 32, 128), BF),
-            shape((27, 4, 4, 64, 128), BF),
+            shape((4, 2, 16, 512), F32),
+            shape((27, 32, 128), F32),
+            shape((27, 64, 128), F32),
         ),
         in_specs=vmem(1) + anywhere(1) + vmem(1) + anywhere(1) + vmem(2),
-        out_specs=tuple(vmem(4) + anywhere(4)),
+        out_specs=tuple(vmem(4)),
         scratch_shapes=[
             pltpu.VMEM((6, 18, 16, 512), BF),
             pltpu.VMEM((8, 6, 18, 16, 128), BF),
             pltpu.VMEM((27, 4, 4, 32, 128), BF),
             pltpu.VMEM((27, 4, 4, 64, 128), BF),
             pltpu.VMEM((1024, 384), F32),
-            dma(2, 5, 4), dma(2, 5, 4), dma(3, 2, 5, 4), dma(3, 2, 5, 4),
-            dma(2), dma(2), dma(2), dma(2),
-            dma(4), dma(4), dma(4), dma(4), dma(3, 4), dma(3, 4), dma(3, 4), dma(3, 4),
-            dma(8),
-        ],
-        compiler_params=pltpu.CompilerParams(
-            collective_id=0, has_side_effects=True, vmem_limit_bytes=VMEM_BYTES
-        ),
-        cost_estimate=pl.CostEstimate(flops=flops, bytes_accessed=40_000_000, transcendentals=600_000),
-    )(volume, w_first, b_first.reshape(1, 128), w_second, b_second.reshape(1, 128), cotangent)
-    grad_input, grad_first, grad_second = pl.pallas_call(
-        backward_kernel,
-        name="backward",
-        out_shape=(
-            shape((4, 2, 16, 512), F32),
-            shape((27, 32, 128), F32),
-            shape((27, 64, 128), F32),
-        ),
-        in_specs=vmem(3) + anywhere(1) + vmem(1) + anywhere(2),
-        out_specs=tuple(vmem(3)),
-        scratch_shapes=[
-            pltpu.VMEM((6, 18, 16, 512), BF),
-            pltpu.VMEM((27, 4, 4, 32, 128), BF),
-            pltpu.VMEM((27, 4, 4, 64, 128), BF),
+            pltpu.VMEM((4, 256, 128), F32),
             pltpu.VMEM((6, 18, 16, 384), BF),
             pltpu.VMEM((6, 18, 16, 384), BF),
             pltpu.VMEM((384, 1024), BF),
+            pltpu.VMEM((384, 1024), BF),
             pltpu.VMEM((2, 16, 16, 128), BF),
             pltpu.VMEM((2, 16, 16, 128), BF),
-            pltpu.VMEM((27, 4, 4, 64, 128), BF),
-            pltpu.VMEM((9, 2, 3, 2, 64, 128), BF),
-            pltpu.VMEM((9, 2, 3, 4, 64, 128), BF),
-            pltpu.VMEM((9, 3, 4, 64, 128), BF),
-            pltpu.VMEM((9, 2, 3, 32, 128), BF),
-            pltpu.VMEM((9, 2, 3, 64, 128), BF),
-            pltpu.VMEM((3, 4, 64, 128), F32),
-            pltpu.VMEM((27, 4, 4, 32, 128), BF),
-            pltpu.VMEM((9, 2, 3, 2, 32, 128), BF),
-            pltpu.VMEM((9, 2, 3, 4, 32, 128), BF),
-            pltpu.VMEM((9, 3, 4, 32, 128), BF),
-            pltpu.VMEM((9, 2, 3, 16, 128), BF),
-            pltpu.VMEM((9, 2, 3, 32, 128), BF),
-            pltpu.VMEM((3, 4, 32, 128), F32),
+            *half_banks(64),
+            *half_banks(32),
             pltpu.VMEM((4, 1024, 128), F32),
             pltpu.VMEM((4, 2, 1024, 128), BF),
             pltpu.VMEM((4, 1024, 128), BF),
@@ -842,18 +785,21 @@
             pltpu.VMEM((4, 4, 2, 16, 512), BF),
             pltpu.VMEM((4, 4, 2, 16, 512), BF),
             pltpu.VMEM((3, 4, 2, 16, 512), BF),
+            dma(2, 5, 4), dma(2, 5, 4), dma(3, 2, 5, 4), dma(3, 2, 5, 4),
+            dma(2), dma(2), dma(2), dma(2),
+            dma(4), dma(4), dma(4), dma(4), dma(3, 4), dma(3, 4), dma(3, 4), dma(3, 4),
+            dma(3),
             dma(9, 4), dma(9, 4), dma(9, 4), dma(9, 4),
             dma(9, 4), dma(9, 4), dma(9, 4), dma(9, 4),
             dma(2), dma(2), dma(2), dma(2),
             dma(4), dma(4), dma(3), dma(3),
             dma(1), dma(1), dma(3), dma(3),
-            dma(4),
         ],
         compiler_params=pltpu.CompilerParams(
-            collective_id=1, has_side_effects=True, vmem_limit_bytes=VMEM_BYTES
+            collective_id=0, has_side_effects=True, vmem_limit_bytes=VMEM_BYTES
         ),
-        cost_estimate=pl.CostEstimate(flops=2 * flops, bytes_accessed=40_000_000, transcendentals=0),
-    )(stacked, flipped, slope, u1, u2, f1, f2)
+        cost_estimate=pl.CostEstimate(flops=3 * flops, bytes_accessed=8_000_000, transcendentals=600_000),
+    )(volume, w_first, b_first.reshape(1, 128), w_second, b_second.reshape(1, 128), cotangent)
     results = (features, grad_input, grad_first, grad_second)
     return pl.pallas_call(
         hand_over,

time: 155 us -> 147 us (0.948)
  Pallas kernels: 154 us -> 147 us
    pallas_call x2 -> x1, Pallas kernels: 151 us -> 144 us  [local(): pl.pallas_call(step_kernel, name='forward_backward', out_shape=(shape((4,...]
where the time goes in v4:
time: 147 us
  Pallas kernels  147 us (100%)
    pallas_call x1, Pallas kernels, local(): pl.pallas_call(step_kernel, name='forward_backward', out_shape=(shape((4,...  144 us

profile of v4, /device:TPU:0, one launch (start us, length us, event | category | flops | bytes accessed | tf_op | source)
XLA Modules:
  0.0 147.3 jit_solution(2820994052673085556)
XLA Ops:
  0.6 143.9 %forward_backward.1 = (bf16[4,16,16,128]{3,2,1,0:T(8,128)(2,1)}, f32[4,2,16,512]{3,2,1,0:T(8,128)}, f32[27,32,128]{2,1,0:T(8,128)}, f32[27,64,128]{2,1,0:T(8,128)}) custom-call(bf16[4,2,16,512]{3,2,1,0:T(8,128)(2,1)} %vol.1, bf16[27,32,128]{2,1,0:T(8,128)(2,1)} %w1.1, f32[1,128]{1,0:T(1,128)} %bitcast.2, bf16[27,64,128]{2,1,0:T(8,128)(2,1)} %w2.1, ...), custom_call_target="tpu_custom_call" | custom-call | flops 32614907904 | bytes 8000000 | tf_op jit(solution)/shard_map/forward_backward/pallas_call | solution.py:752
  144.6 2.7 %hand_over.1 = (bf16[4,16,16,128]{3,2,1,0:T(8,128)(2,1)}, f32[4,2,16,512]{3,2,1,0:T(8,128)}, f32[27,32,128]{2,1,0:T(8,128)}, f32[27,64,128]{2,1,0:T(8,128)}) custom-call(bf16[4,16,16,128]{3,2,1,0:T(8,128)(2,1)} %get-tuple-element.8.refs_0_, f32[4,2,16,512]{3,2,1,0:T(8,128)} %get-tuple-element.9.refs_1_, f32[27,32,128]{2,1,0:T(8,128)} %get-tuple-element.10.refs_2_, ...), custom_call_target="tpu_custom_call" | custom-call | tf_op jit(solution)/shard_map/hand_over/pallas_call | solution.py:804

commit v5 on v4

--- a/solution.py
+++ b/solution.py
@@ -561,9 +561,9 @@
         scatter2.start1(j)
 
     every_chunk(second_chunk, 0, 6)
-    take_rims(halo2, rim2, adj2)
     scatter2.relay1(0)
     scatter2.relay1(1)
+    take_rims(halo2, rim2, adj2)
 
     def hidden_to_sibling(n):
         return send(hid_bf.at[n, 1 - core], hid_sib.at[n], hss.at[n], hsr.at[n], sibling)
@@ -579,6 +579,11 @@
     def hidden_columns(i, _):
         n = lax.rem(y + 1 + i, 4)
         pl.when(i < 3)(lambda: second_chunk(jnp.minimum(6 + i, 8)))
+
+        @pl.when(i == 1)
+        def _():
+            scatter2.relay1(3)
+
         value = back_columns(adj2, lambda k: f2[k, n].reshape(256, 128))
         low, high = value[:, :128], value[:, 128:]
         hid_bf[n, 0] = low.astype(BF)
@@ -593,20 +598,29 @@
             hid_sum[before] = hidden_pair(before).astype(BF)
             hidden_to_y(d).start()
 
-        @pl.when(i < 3)
-        def _():
-            scatter2.relay1(2 * jnp.minimum(i, 2) + 2)
-            scatter2.relay1(2 * jnp.minimum(i, 2) + 3)
-
-        pl.when(i > 0)(lambda: scatter2.start2(jnp.maximum(i - 1, 0)))
+        @pl.when(i == 0)
+        def _():
+            scatter2.relay1(2)
+
+        @pl.when(i == 2)
+        def _():
+            scatter2.start2(0)
+            scatter2.relay1(4)
+            scatter2.relay1(5)
+            scatter2.relay1(6)
+            scatter2.relay1(7)
+
         return 0
 
     lax.fori_loop(0, 4, hidden_columns, 0)
     hid_own[y] = hidden_pair(y)
 
+    scatter2.start2(1)
+    scatter2.start2(2)
     scatter2.start2(3)
     scatter2.start2(4)
     scatter2.relay1(8)
+    scatter2.relay2(0)
     for d in RING:
         hidden_to_y(d).wait_recv()
     for p in range(4):
@@ -619,8 +633,6 @@
         s, c, adj1.at[1, 1:17, :, middle], adj1.at[4, 1:17, :, middle], rim1.at[0], rim1.at[1], h1s, h1r
     )
     halo1.start()
-    scatter2.relay2(0)
-    scatter2.relay2(1)
 
     def first_chunk(j):
         a, b = lax.div(j, 3), lax.rem(j, 3)
@@ -632,12 +644,29 @@
 
     def first_step(j):
         first_chunk(j)
-        pl.when(j > 4)(lambda: scatter1.relay1(jnp.maximum(j - 5, 0)))
+
+        @pl.when(j == 0)
+        def _():
+            scatter2.relay2(1)
+
+        @pl.when(j == 1)
+        def _():
+            scatter2.relay2(2)
+
+        @pl.when(j == 5)
+        def _():
+            scatter1.relay1(0)
+
+        @pl.when(j == 7)
+        def _():
+            scatter2.start2(5)
+            scatter1.relay1(1)
+            scatter1.relay1(2)
 
     every_chunk(first_step)
-    scatter2.start2(5)
+    scatter1.relay1(3)
+    scatter1.relay1(4)
     take_rims(halo1, rim1, adj1)
-    scatter1.relay1(4)
     for n in range(2):
         value = back_columns(adj1, lambda k: f1[k, 2 * n : 2 * n + 2].reshape(256, 128))
         value = value.reshape(4, 4, 2, 2, 16, 256)
@@ -645,10 +674,9 @@
         inp_own[:, :, :, :, :, columns] = value
         inp_bf[:, :, :, :, :, columns] = value.astype(BF)
         if n == 0:
+            scatter1.relay1(5)
             scatter1.start2(0)
-            for j in (5, 6, 7):
-                scatter1.relay1(j)
-            scatter2.start2(6)
+            scatter1.relay1(6)
     to_sibling = send(inp_bf.at[:, :, 1 - core], inp_sib, iss.at[0], isr.at[0], sibling)
     to_sibling.start()
 
@@ -656,12 +684,17 @@
         n = lax.rem(y + d, 4)
         return send(inp_sum.at[n], inp_got.at[d - 1], iys.at[d - 1], iyr.at[d - 1], (s, n * 2 + core))
 
+    scatter1.relay1(7)
+    scatter2.relay2(3)
+    scatter2.start2(6)
     scatter1.relay1(8)
-    scatter2.relay2(2)
-    scatter2.relay2(3)
     scatter1.start2(1)
     scatter1.start2(2)
+    scatter1.start2(3)
     scatter2.start2(7)
+    scatter2.relay2(4)
+    scatter2.finish(0)
+    scatter1.start2(4)
     to_sibling.wait_recv()
     for d in (1, 3, 2, 0):
         n = lax.rem(y + d, 4)
@@ -671,36 +704,47 @@
             input_to_y(d).start()
         else:
             grad_in[...] = pair
-    for j in (3, 4, 5):
-        scatter1.start2(j)
-    scatter1.relay2(0)
-    scatter2.relay2(4)
-    scatter1.relay2(1)
-    scatter2.start2(8)
+    scatter1.start2(5)
     scatter1.start2(6)
-    scatter1.relay2(2)
     scatter2.relay2(5)
     scatter1.start2(7)
+    scatter2.start2(8)
+    scatter2.relay2(6)
+    scatter2.finish(1)
+    scatter2.finish(2)
+    scatter1.relay2(0)
+    scatter1.start2(8)
+    scatter1.relay2(1)
+    scatter1.relay2(2)
     scatter1.relay2(3)
-    scatter2.relay2(6)
-    scatter1.start2(8)
     scatter1.relay2(4)
+    scatter2.relay2(7)
+    scatter2.finish(3)
     scatter1.relay2(5)
-    scatter2.relay2(7)
     scatter1.relay2(6)
+    scatter1.relay2(7)
     scatter2.relay2(8)
-    scatter1.relay2(7)
+    scatter1.finish(0)
     scatter1.relay2(8)
-    every_chunk(scatter2.finish, 0, 7)
+    scatter2.finish(4)
+    scatter1.finish(1)
+    scatter1.finish(2)
+    scatter1.finish(3)
+    scatter2.finish(5)
+    scatter2.finish(6)
+    scatter1.finish(4)
+    scatter1.finish(5)
     for d in RING:
         input_to_y(d).wait_recv()
     value = grad_in[...]
     for d in range(3):
         value = value + inp_got[d].astype(F32)
     grad_in[...] = value
-    every_chunk(scatter1.finish, 0, 6)
-    every_chunk(scatter2.finish, 7, 9)
-    every_chunk(scatter1.finish, 6, 9)
+    scatter1.finish(6)
+    scatter1.finish(7)
+    scatter2.finish(7)
+    scatter1.finish(8)
+    scatter2.finish(8)
 
     halo2.wait_send()
     halo1.wait_send()

time: 147 us -> 146 us (level)
  Pallas kernels: 147 us -> 145 us
    pallas_call x1, Pallas kernels: 144 us -> 142 us  [local(): pl.pallas_call(step_kernel, name='forward_backward', out_shape=(shape((4,...]
where the time goes in v5:
time: 146 us
  Pallas kernels  145 us (99%)
    pallas_call x1, Pallas kernels, local(): pl.pallas_call(step_kernel, name='forward_backward', out_shape=(shape((4,...  142 us

profile of v5, /device:TPU:0, one launch (start us, length us, event | category | flops | bytes accessed | tf_op | source)
XLA Modules:
  0.0 145.6 jit_solution(9155352335121829630)
XLA Ops:
  0.6 142.2 %forward_backward.1 = (bf16[4,16,16,128]{3,2,1,0:T(8,128)(2,1)}, f32[4,2,16,512]{3,2,1,0:T(8,128)}, f32[27,32,128]{2,1,0:T(8,128)}, f32[27,64,128]{2,1,0:T(8,128)}) custom-call(bf16[4,2,16,512]{3,2,1,0:T(8,128)(2,1)} %vol.1, bf16[27,32,128]{2,1,0:T(8,128)(2,1)} %w1.1, f32[1,128]{1,0:T(1,128)} %bitcast.2, bf16[27,64,128]{2,1,0:T(8,128)(2,1)} %w2.1, ...), custom_call_target="tpu_custom_call" | custom-call | flops 32614907904 | bytes 8000000 | tf_op jit(solution)/shard_map/forward_backward/pallas_call | solution.py:796
  142.8 2.7 %hand_over.1 = (bf16[4,16,16,128]{3,2,1,0:T(8,128)(2,1)}, f32[4,2,16,512]{3,2,1,0:T(8,128)}, f32[27,32,128]{2,1,0:T(8,128)}, f32[27,64,128]{2,1,0:T(8,128)}) custom-call(bf16[4,16,16,128]{3,2,1,0:T(8,128)(2,1)} %get-tuple-element.8.refs_0_, f32[4,2,16,512]{3,2,1,0:T(8,128)} %get-tuple-element.9.refs_1_, f32[27,32,128]{2,1,0:T(8,128)} %get-tuple-element.10.refs_2_, ...), custom_call_target="tpu_custom_call" | custom-call | tf_op jit(solution)/shard_map/hand_over/pallas_call | solution.py:848
